TPU v7x, 128 devices: a whole 4x4x4 slice. The times are simulated.
128 devices in a mesh: section: 4 (over z), expert: 4 (over x), tensor: 8 (over y, core).
Axes of the slice: x: 4, y: 4, z: 4, core: 2. Of those that a mesh axis runs over, the one named last changes fastest.
Arguments:
- update: bfloat16 [8, 7168, 2048], P('section', 'tensor', 'expert'), may hold values from -4 to 4
- residual: float32 [8, 7168, 2048], P('section', 'tensor', 'expert'), may hold values from -2 to 2
- kept_blocks: int32 [8, 8, 8, 4], P('section', 'tensor', 'expert'), may hold values from 0 to 13, as said below
- kept_count: int32 [8], replicated, may hold values from 2 to 4, as said below
- serving_slot: int32 [8], replicated, may hold values from 0 to 7, as said below
- served_up: bfloat16 [4, 8, 7168, 2048], P('section', 'expert', None, 'tensor'), may hold values from -6 to 6
Outputs:
- served_new: bfloat16 [4, 8, 7168, 2048], P('section', 'expert', None, 'tensor')
- residual_new: float32 [8, 7168, 2048], P('section', 'tensor', 'expert')
Inputs may be any that keep to these rules, and one draw needn't show every extreme that they name: `kept_blocks`: the 4 entries of one row differ; each names one of the group's 14 blocks in row-major order: block row within the row range times (2) plus block column within the group's 256 hidden units. Expert e uses the first kept_count[e] slots of each of its rows of kept_blocks; some expert uses all 4. A permutation: expert e is served at position serving_slot[e], on device serving_slot[e] // 2 of the expert axis; experts trained on one section (equal e // 2) are served on different devices.
All inputs are finite; a program needn't handle non-finite values.
Results may differ from a plain program's by a relative error of at most 0.0039.
Values may be sent and summed in bfloat16 or wider, within the bound.
A program may use at most 128 MiB of HBM per device.

v0:
```python
import jax
import jax.numpy as jnp
from jax import lax
from jax.sharding import PartitionSpec as P

BLK = 128


def as_sent(value):
    return jax.tree.map(lambda a: a.astype(jnp.bfloat16) if a.dtype == jnp.float32 else a, value)


def take_blocks(source, starts):
    numbers = lax.GatherDimensionNumbers(
        offset_dims=(1, 2), collapsed_slice_dims=(0,), start_index_map=(0, 1, 2)
    )
    return lax.gather(source, starts, numbers, (1, BLK, BLK), mode="fill", fill_value=0)


def on_device(update, residual, kept_blocks, kept_count, serving_slot, served_up):
    sections = lax.axis_size("section")
    experts = lax.axis_size("expert")
    tensors = lax.axis_size("tensor")
    section_index = lax.axis_index("section")
    expert_index = lax.axis_index("expert")
    own_experts, own_rows, own_columns = update.shape
    groups_own = kept_blocks.shape[2]
    keep_slots = kept_blocks.shape[3]
    width_group = own_columns // groups_own
    group_blocks = width_group // BLK
    row_blocks = own_rows // BLK
    experts_here = served_up.shape[1]
    window_experts = kept_count.shape[0]
    per_slice = experts * groups_own // tensors
    change = update.astype(jnp.float32) + residual
    rounded = change.astype(jnp.bfloat16)
    every_expert = jnp.arange(window_experts, dtype=jnp.int32)
    trained = section_index * own_experts + jnp.arange(own_experts, dtype=jnp.int32)
    is_trained = every_expert[None, :] == trained[:, None]
    keep_counts = jnp.sum(jnp.where(is_trained, kept_count[None, :], 0), axis=1)
    trained_slot = jnp.sum(jnp.where(is_trained, serving_slot[None, :], 0), axis=1)
    own_codes = kept_blocks[:, 0]
    slot_ids = jnp.arange(keep_slots, dtype=jnp.int32)
    in_use = slot_ids[None, None, :] < keep_counts[:, None, None]
    block_ids = jnp.arange(row_blocks * group_blocks, dtype=jnp.int32)
    covered = jnp.any(
        (own_codes[:, :, None, :] == block_ids[None, None, :, None]) & in_use[:, :, None, :], axis=3
    )
    covered = covered.reshape(own_experts, groups_own, row_blocks, group_blocks).transpose(
        0, 2, 1, 3
    )
    covered = covered.reshape(own_experts, row_blocks, groups_own * group_blocks)
    column_mask = jnp.repeat(covered, BLK, axis=2)
    change_rows = change.reshape(own_experts, row_blocks, BLK, own_columns)
    rounded_rows = rounded.reshape(change_rows.shape)
    residual_new = change_rows - jnp.where(
        column_mask[:, :, None, :], rounded_rows.astype(jnp.float32), 0.0
    )
    residual_new = residual_new.reshape(own_experts, own_rows, own_columns)
    block_row = own_codes // group_blocks
    block_col = (
        jnp.arange(groups_own, dtype=jnp.int32)[None, :, None] * group_blocks
        + own_codes % group_blocks
    )
    expert_pick = jnp.broadcast_to(
        jnp.arange(own_experts, dtype=jnp.int32)[:, None, None], own_codes.shape
    )
    pick_starts = jnp.stack(
        [expert_pick.reshape(-1), block_row.reshape(-1) * BLK, block_col.reshape(-1) * BLK], axis=1
    )
    chosen_blocks = take_blocks(rounded, pick_starts).reshape(own_codes.shape + (BLK, BLK))
    chosen_blocks = jnp.where(in_use[..., None, None], chosen_blocks, jnp.zeros((), jnp.bfloat16))
    send_codes = jnp.where(in_use, own_codes, -1)
    target_device = trained_slot // experts_here
    device_ids = jnp.arange(experts, dtype=jnp.int32)
    goes_there = target_device[None, :] == device_ids[:, None]
    gets_expert = jnp.any(goes_there, axis=1)
    source_expert = jnp.sum(
        jnp.where(goes_there, jnp.arange(own_experts, dtype=jnp.int32)[None, :], 0), axis=1
    )
    payload = jnp.where(
        gets_expert[:, None, None, None, None],
        chosen_blocks[source_expert],
        jnp.zeros((), jnp.bfloat16),
    )
    payload_codes = jnp.where(gets_expert[:, None, None], send_codes[source_expert], -1)
    copies = jnp.broadcast_to(payload[None], (sections,) + payload.shape)
    copies = copies.reshape((sections * experts,) + payload.shape[1:])
    copy_codes = jnp.broadcast_to(payload_codes[None], (sections,) + payload_codes.shape)
    copy_codes = copy_codes.reshape((sections * experts,) + payload_codes.shape[1:])
    shifted, shifted_codes = (
        lax.all_to_all(
            as_sent(copies), ("section", "expert"), split_axis=0, concat_axis=1, tiled=True
        ).astype(copies.dtype),
        lax.all_to_all(copy_codes, ("section", "expert"), split_axis=0, concat_axis=1, tiled=True),
    )
    shifted = shifted.reshape(sections, tensors, per_slice, keep_slots, BLK, BLK)
    shifted_codes = shifted_codes.reshape(sections, tensors, per_slice, keep_slots)
    arrived, arrived_codes = (
        lax.all_to_all(as_sent(shifted), "tensor", split_axis=1, concat_axis=1, tiled=True).astype(
            shifted.dtype
        ),
        lax.all_to_all(shifted_codes, "tensor", split_axis=1, concat_axis=1, tiled=True),
    )
    source_sections = jnp.arange(sections, dtype=jnp.int32)
    served_here = serving_slot // experts_here == expert_index
    trained_by = every_expert // own_experts
    from_section = served_here[None, :] & (trained_by[None, :] == source_sections[:, None])
    has_expert = jnp.any(from_section, axis=1)
    slot_here = jnp.sum(jnp.where(from_section, serving_slot[None, :] % experts_here, 0), axis=1)
    slot_ids_here = jnp.arange(experts_here, dtype=jnp.int32)
    select_slot = ((slot_ids_here[:, None] == slot_here[None, :]) & has_expert[None, :]).astype(
        jnp.bfloat16
    )
    position_ids = jnp.arange(row_blocks * group_blocks, dtype=jnp.int32)
    one_hot = (arrived_codes[..., None] == position_ids).astype(jnp.bfloat16)
    grid = jnp.einsum(
        "stpjb,stpjxy->stpbxy", one_hot, arrived, preferred_element_type=jnp.float32
    ).astype(jnp.bfloat16)
    grid = grid.reshape(sections, tensors, per_slice, row_blocks, group_blocks, BLK, BLK)
    by_slot = jnp.einsum(
        "es,stpabxy->etaxpby", select_slot, grid, preferred_element_type=jnp.float32
    )
    by_slot = by_slot.reshape(
        experts_here, tensors * row_blocks * BLK, per_slice * group_blocks * BLK
    )
    weights = (served_up[0].astype(jnp.float32) + by_slot).astype(jnp.bfloat16)
    return (weights[None], residual_new)


def solution(mesh):
    return jax.shard_map(
        on_device,
        mesh=mesh,
        in_specs=(
            P("section", "tensor", "expert"),
            P("section", "tensor", "expert"),
            P("section", "tensor", "expert", None),
            P(),
            P(),
            P("section", "expert", None, "tensor"),
        ),
        out_specs=(P("section", "expert", None, "tensor"), P("section", "tensor", "expert")),
        check_vma=False,
    )
```

profile of v0, /device:TPU:1, one launch (start us, length us, event | category | flops | bytes accessed | tf_op | source)
XLA Modules:
  0.0 315.7 jit_solution(2346464781384651268)
XLA Ops:
  3.8 8.4 %all-to-all-start = ((s32[16,2,4]{2,1,0:T(2,128)}), s32[16,2,4]{2,1,0:T(2,128)S(1)}, u32[]{:S(2)}, u32[]{:S(2)}) async-start(s32[16,2,4]{2,1,0:T(2,128)} %bitcast.3), calls=%async_computation | async-start | bytes 32768 | tf_op jit(solution)/shard_map/all_to_all | solution.py:95
  14.5 5.3 %select_subtract_fusion = (f32[2,896,512]{2,1,0:T(8,128)}, bf16[2,896,512]{2,1,0:T(8,128)(2,1)S(1)}) fusion(f32[2,896,512]{2,1,0:T(8,128)} %param.7, bf16[2,896,512]{2,1,0:T(8,128)(2,1)} %param.6, pred[2,7,512]{2,1,0:T(8,128)(4,1)S(1)} %broadcast_in_dim.181), kind=kLoop, calls=%fused_computation.13 | loop fusion | flops 5505024 | bytes 11017216 | tf_op jit(solution)/shard_map/sub | solution.py:56
  19.8 42.9 %while.1 = (s32[]{:T(128)}, bf16[2,896,512]{2,1,0:T(8,128)(2,1)S(1)}, s32[16,3]{0,1:T(4,128)S(1)}, bf16[16,128,128]{2,1,0:T(8,128)(2,1)S(1)}, s32[]{:T(128)}) while((s32[]{:T(128)}, bf16[2,896,512]{2,1,0:T(8,128)(2,1)S(1)}, s32[16,3]{0,1:T(4,128)S(1)}, bf16[16,128,128]{2,1,0:T(8,128)(2,1)S(1)}, s32[]{:T(128)}) %tuple.32), condition=%wide.while_cond, body=%wide.while_body.sunk | while | flops 2 | bytes 65665 | solution.py:17
  20.5 2.0 dynamic-slice_dynamic-update-slice_fusion.2
  23.2 2.0 dynamic-slice_dynamic-update-slice_fusion.2
  25.8 2.0 dynamic-slice_dynamic-update-slice_fusion.2
  28.5 2.0 dynamic-slice_dynamic-update-slice_fusion.2
  31.2 2.0 dynamic-slice_dynamic-update-slice_fusion.2
  33.9 2.0 dynamic-slice_dynamic-update-slice_fusion.2
  36.6 2.0 dynamic-slice_dynamic-update-slice_fusion.2
  39.2 2.0 dynamic-slice_dynamic-update-slice_fusion.2
  63.9 3.1 broadcast_in_dim.177
  67.0 6.7 %all-to-all-start.2 = ((bf16[16,2,4,128,128]{4,3,2,1,0:T(8,128)(2,1)}), bf16[16,2,4,128,128]{4,3,2,1,0:T(8,128)(2,1)}, u32[]{:S(2)}, u32[]{:S(2)}) async-start(bf16[16,2,4,128,128]{4,3,2,1,0:T(8,128)(2,1)} %bitcast.47), calls=%async_computation.2 | async-start | bytes 8388608 | tf_op jit(solution)/shard_map/all_to_all | solution.py:92
  74.3 60.0 %all-to-all-done.2 = bf16[16,2,4,128,128]{4,3,2,1,0:T(8,128)(2,1)} async-done(((bf16[16,2,4,128,128]{4,3,2,1,0:T(8,128)(2,1)}), bf16[16,2,4,128,128]{4,3,2,1,0:T(8,128)(2,1)}, u32[]{:S(2)}, u32[]{:S(2)}) %all-to-all-start.2) | async-done | bytes 4194336 | tf_op jit(solution)/shard_map/all_to_all | solution.py:92
  134.3 6.9 %all-to-all-start.1 = ((s32[4,8,1,4]{3,0,2,1:T(4,128)}), s32[4,8,1,4]{3,0,2,1:T(4,128)S(1)}, u32[]{:S(2)}, u32[]{:S(2)}) async-start(s32[4,8,1,4]{3,0,2,1:T(4,128)} %copy.59), calls=%async_computation.1 | async-start | bytes 32768 | tf_op jit(solution)/shard_map/all_to_all | solution.py:103
  141.2 8.2 %copy.62 = bf16[4,8,1,4,128,128]{5,3,4,0,2,1:T(4,128)(2,1)} copy(bf16[4,8,1,4,128,128]{5,4,3,1,0,2:T(8,128)(2,1)} %bitcast.10) | data formatting | bytes 8388608 | tf_op jit(solution)/shard_map/reshape | solution.py:97
  149.3 4.9 %all-to-all-start.3 = ((bf16[4,8,1,4,128,128]{5,3,4,0,2,1:T(4,128)(2,1)}), bf16[4,8,1,4,128,128]{5,3,4,0,2,1:T(4,128)(2,1)}, u32[]{:S(2)}, u32[]{:S(2)}) async-start(bf16[4,8,1,4,128,128]{5,3,4,0,2,1:T(4,128)(2,1)} %copy.62), calls=%async_computation.3 | async-start | bytes 8388608 | tf_op jit(solution)/shard_map/all_to_all | solution.py:100
  154.5 48.6 %all-to-all-done.3 = bf16[4,8,1,4,128,128]{5,3,4,0,2,1:T(4,128)(2,1)} async-done(((bf16[4,8,1,4,128,128]{5,3,4,0,2,1:T(4,128)(2,1)}), bf16[4,8,1,4,128,128]{5,3,4,0,2,1:T(4,128)(2,1)}, u32[]{:S(2)}, u32[]{:S(2)}) %all-to-all-start.3) | async-done | bytes 4194336 | tf_op jit(solution)/shard_map/all_to_all | solution.py:100
  203.2 9.1 %convolution_convert_fusion = bf16[4,8,14,128,128]{4,2,3,1,0:T(8,128)(2,1)S(1)} fusion(bf16[4,8,1,4,128,128]{5,3,4,0,2,1:T(4,128)(2,1)} %all-to-all-done.3, s32[4,8,4]{2,1,0:T(8,128)S(1)} %copy.61), kind=kOutput, calls=%fused_computation.10 | convolution fusion | flops 66062080 | bytes 18874880 | tf_op jit(solution)/shard_map/stpjb,stpjxy->stpbxy/dot_general | solution.py:117
  212.2 10.8 %copy.64 = bf16[4,8,14,128,128]{4,3,2,1,0:T(8,128)(2,1)} copy(bf16[4,8,14,128,128]{4,2,3,1,0:T(8,128)(2,1)S(1)} %convolution_convert_fusion) | data formatting | bytes 29360128 | tf_op jit(solution)/shard_map/convert_element_type | solution.py:119
  223.1 41.0 %fusion.4 = f32[2,8,7,128,1,2,128]{6,0,3,5,2,1,4:T(2,128)} fusion(bf16[4,8,7,2,128,128]{5,4,3,2,1,0:T(8,128)(2,1)} %bitcast.46, pred[4]{0:T(512)(128)(4,1)S(1)} %fusion.19, s32[4]{0:T(128)S(1)} %select_reduce_fusion), kind=kOutput, calls=%fused_computation.9 | convolution fusion | flops 29360144 | bytes 29360148 | tf_op jit(solution)/shard_map/es,stpabxy->etaxpby/dot_general | solution.py:121
  264.1 24.4 %copy.66 = f32[2,8,7,128,1,2,128]{6,5,4,3,2,1,0:T(2,128)S(1)} copy(f32[2,8,7,128,1,2,128]{6,0,3,5,2,1,4:T(2,128)} %fusion.4) | data formatting | bytes 29360128 | tf_op jit(solution)/shard_map/es,stpabxy->etaxpby/transpose | solution.py:121
  288.5 17.7 %fusion.1 = bf16[1,2,7168,256]{3,0,2,1:T(2,128)(2,1)} fusion(f32[1,2,7168,256]{3,0,2,1:T(1,128)S(1)} %bitcast.45, bf16[1,2,7168,256]{3,2,1,0:T(8,128)(2,1)} %param.11), kind=kLoop, calls=%fused_computation.6 | loop fusion | flops 11010048 | bytes 29360128 | tf_op jit(solution)/shard_map/convert_element_type | solution.py:127
  306.2 9.5 %copy.69 = bf16[1,2,7168,256]{3,2,1,0:T(8,128)(2,1)} copy(bf16[1,2,7168,256]{3,0,2,1:T(2,128)(2,1)} %fusion.1) | data formatting | bytes 14680064
  (85 shorter events, 34.2 us)
Async XLA Ops:
  3.8 60.2 %all-to-all-start = ((s32[16,2,4]{2,1,0:T(2,128)}), s32[16,2,4]{2,1,0:T(2,128)S(1)}, u32[]{:S(2)}, u32[]{:S(2)}) async-start(s32[16,2,4]{2,1,0:T(2,128)} %bitcast.3), calls=%async_computation | async-start | bytes 32768 | tf_op jit(solution)/shard_map/all_to_all | solution.py:95
  14.5 48.2 %copy-start.1 = (s32[3]{0:T(128)S(1)}, s32[3]{0:T(128)}, u32[]{:S(2)}) copy-start(s32[3]{0:T(128)} %constant.86.clone.1) | copy-start | bytes 40
  67.0 67.3 %all-to-all-start.2 = ((bf16[16,2,4,128,128]{4,3,2,1,0:T(8,128)(2,1)}), bf16[16,2,4,128,128]{4,3,2,1,0:T(8,128)(2,1)}, u32[]{:S(2)}, u32[]{:S(2)}) async-start(bf16[16,2,4,128,128]{4,3,2,1,0:T(8,128)(2,1)} %bitcast.47), calls=%async_computation.2 | async-start | bytes 8388608 | tf_op jit(solution)/shard_map/all_to_all | solution.py:92
  134.3 15.0 %all-to-all-start.1 = ((s32[4,8,1,4]{3,0,2,1:T(4,128)}), s32[4,8,1,4]{3,0,2,1:T(4,128)S(1)}, u32[]{:S(2)}, u32[]{:S(2)}) async-start(s32[4,8,1,4]{3,0,2,1:T(4,128)} %copy.59), calls=%async_computation.1 | async-start | bytes 32768 | tf_op jit(solution)/shard_map/all_to_all | solution.py:103
  149.3 4.9 %copy-start = (s32[8]{0:T(128)S(1)}, s32[8]{0:T(128)}, u32[]{:S(2)}) copy-start(s32[8]{0:T(128)} %param.10) | copy-start | bytes 100
  149.3 53.8 %all-to-all-start.3 = ((bf16[4,8,1,4,128,128]{5,3,4,0,2,1:T(4,128)(2,1)}), bf16[4,8,1,4,128,128]{5,3,4,0,2,1:T(4,128)(2,1)}, u32[]{:S(2)}, u32[]{:S(2)}) async-start(bf16[4,8,1,4,128,128]{5,3,4,0,2,1:T(4,128)(2,1)} %copy.62), calls=%async_computation.3 | async-start | bytes 8388608 | tf_op jit(solution)/shard_map/all_to_all | solution.py:100
where the time goes:
time: 317 us; the launch traced here: 316 us
  waiting for transfers between devices  109 us (34%)
  local copies, waits for them, and re-layouts  103 us (32%)
  matrix products  50.1 us (16%)
  starting transfers between devices  26.9 us (8%)
  other arithmetic  26.3 us (8%)
    all_to_all x1, waiting for transfers between devices, on_device(): lax.all_to_all(as_sent(copies), ('section', 'expert'), split_axis=0, conc...  60 us
    all_to_all x1, waiting for transfers between devices, on_device(): lax.all_to_all(as_sent(shifted), 'tensor', split_axis=1, concat_axis=1, t...  48.6 us
    gather x48, local copies, waits for them, and re-layouts  42.6 us
    dot_general x1, matrix products, on_device(): jnp.einsum('es,stpabxy->etaxpby', select_slot, grid, preferred_element_ty...  41 us
    transpose x1, local copies, waits for them, and re-layouts, on_device(): jnp.einsum('es,stpabxy->etaxpby', select_slot, grid, preferred_element_ty...  24.4 us
    convert_element_type x1, other arithmetic, on_device(): weights = (served_up[0].astype(jnp.float32) + by_slot).astype(jnp.bfloat16)  17.7 us
    convert_element_type x1, local copies, waits for them, and re-layouts, on_device(): grid = jnp.einsum('stpjb,stpjxy->stpbxy', one_hot, arrived, preferred_ele...  10.8 us
    unnamed x5, local copies, waits for them, and re-layouts  9.52 us
  transfers between devices with their start and end apart: 4, of which 2 were waited for; matrix products, arithmetic and copies ran while one was open for 19% of the time, Pallas kernels for 0%

commit v1 on v0

v1 whole, which is shorter than its diff:
```python
import functools

import jax
import jax.numpy as jnp
from jax import lax
from jax.experimental import pallas as pl
from jax.experimental.pallas import tpu as pltpu
from jax.sharding import PartitionSpec as P

MESH = pl.DeviceIdType.MESH
BLK = 128
SECTIONS = 4
EXPERTS = 4
TENSORS = 8
OWN = 2
GROUPS = 2
KEEP = 4
ROW_BLOCKS = 7
WINDOW = 8
SLOTS_A = 2
CHUNKS_A = 4
CHUNKS_B = 4
ROWS_A = BLK // CHUNKS_A
SHARE_B = (KEEP - SLOTS_A) * BLK // SECTIONS
ROWS_B = SHARE_B // CHUNKS_B


def own_place():
    return lax.axis_index("section"), lax.axis_index("expert"), lax.axis_index("tensor")


def share_place(section, chunk):
    first = section * SHARE_B + chunk * ROWS_B
    return SLOTS_A + first // BLK, first % BLK


def pack_kernel(update, residual, kept, packed, numbers, upd, res, upd_sem, res_sem):
    picks = [(le, gl, j) for le in range(OWN) for gl in range(GROUPS) for j in range(KEEP)]
    copies = []
    for i, (le, gl, j) in enumerate(picks):
        code = kept[le, 0, gl, j]
        row = pl.multiple_of((code // 2) * BLK, BLK)
        column = pl.multiple_of((gl * 2 + code % 2) * BLK, BLK)
        at = (le, pl.ds(row, BLK), pl.ds(column, BLK))
        copies.append(
            (
                pltpu.make_async_copy(update.at[at], upd.at[i], upd_sem.at[i]),
                pltpu.make_async_copy(residual.at[at], res.at[i], res_sem.at[i]),
            )
        )
        for copy in copies[-1]:
            copy.start()
    lanes = lax.broadcasted_iota(jnp.int32, (1, BLK), 1)
    row = jnp.zeros((1, BLK), jnp.int32)
    for i, (le, gl, j) in enumerate(picks):
        row = jnp.where(lanes == i, kept[le, 0, gl, j], row)
    numbers[...] = row
    for i, (le, gl, j) in enumerate(picks):
        for copy in copies[i]:
            copy.wait()
        packed[le, gl, j] = (upd[i].astype(jnp.float32) + res[i]).astype(jnp.bfloat16)


def pack(update, residual, kept):
    n = OWN * GROUPS * KEEP
    hbm, vmem = pltpu.HBM, pltpu.VMEM
    return pl.pallas_call(
        pack_kernel,
        out_shape=(
            vmem((OWN, GROUPS, KEEP, BLK, BLK), jnp.bfloat16),
            vmem((1, BLK), jnp.int32),
        ),
        in_specs=[pl.BlockSpec(memory_space=m) for m in (hbm, hbm, pltpu.SMEM)],
        out_specs=(pl.BlockSpec(memory_space=vmem),) * 2,
        scratch_shapes=[
            vmem((n, BLK, BLK), jnp.bfloat16),
            vmem((n, BLK, BLK), jnp.float32),
            pltpu.SemaphoreType.DMA((n,)),
            pltpu.SemaphoreType.DMA((n,)),
        ],
        compiler_params=pltpu.CompilerParams(vmem_limit_bytes=16 << 20),
        name="pack",
    )(update, residual, kept)


def push_kernel(
    packed, numbers, update, residual, kept, count, slots, served,
    res_out, staged, fin_a, fin_b, fin_c,
    upd, sel, z_a, s_a, x_a, z_b, s_b, x_b, z_c, x_c,
    load_sem,
    a1_s, a1_r, a2_s, a2_r, a3_s, a3_r,
    b1_s, b1_r, b2_s, b2_r, b3_s, b3_r, b4_s, b4_r,
    c1_s, c1_r, c2_s, c2_r, c3_s, c3_r,
):
    z, x, t = own_place()
    up, down = (z + 1) % SECTIONS, (z + 3) % SECTIONS

    loads = []
    for le in range(OWN):
        loads.append(pltpu.make_async_copy(update.at[le], upd.at[le], load_sem.at[2 * le]))
        loads.append(pltpu.make_async_copy(residual.at[le], res_out.at[le], load_sem.at[2 * le + 1]))
    for load in loads:
        load.start()
    stage = pltpu.make_async_copy(served.at[0], staged, load_sem.at[4])
    stage.start()

    for p in range(WINDOW):
        for e in range(WINDOW):
            here = (slots[e] == p).astype(jnp.float32)
            sel[p, e] = jnp.full(sel.shape[2:], here, jnp.float32).astype(sel.dtype)
    z_c[z] = numbers[...]

    barrier = pltpu.get_barrier_semaphore()
    for d in range(1, SECTIONS):
        pl.semaphore_signal(barrier, inc=1, device_id=((z + d) % SECTIONS, x, t), device_id_type=MESH)
    for d in range(1, EXPERTS):
        pl.semaphore_signal(barrier, inc=1, device_id=(z, (x + d) % EXPERTS, t), device_id_type=MESH)
    for d in range(1, TENSORS):
        pl.semaphore_signal(barrier, inc=1, device_id=(z, x, (t + d) % TENSORS), device_id_type=MESH)

    pl.semaphore_wait(barrier, SECTIONS + EXPERTS + TENSORS - 3)

    def remote(src, dst, send, recv, to):
        return pltpu.make_async_remote_copy(
            src_ref=src, dst_ref=dst, send_sem=send, recv_sem=recv, device_id=to, device_id_type=MESH
        )

    def b1(q, d):
        to = (z + d) % SECTIONS
        slot, row = share_place(to, q)
        row = pl.multiple_of(row, ROWS_B)
        return remote(
            packed.at[:, :, slot, pl.ds(row, ROWS_B)], z_b.at[q, z], b1_s.at[q, d], b1_r.at[q, d], (to, x, t)
        )

    def ring(buffer, send, recv, q, half, leap, going_up):
        own = (z + SECTIONS - leap) % SECTIONS if going_up else (z + leap) % SECTIONS
        n = buffer.shape[2] // 2
        ref = buffer.at[q, own, pl.ds(half * n, n)]
        i = 2 * (0 if going_up else 1) + half if leap == 0 else 4 + half
        return remote(ref, ref, send.at[q, i], recv.at[q, i], (up if going_up else down, x, t))

    def a1(q, half, leap, going_up):
        return ring(z_a, a1_s, a1_r, q, half, leap, going_up)

    def b4(q, half, leap, going_up):
        return ring(fin_b, b4_s, b4_r, q, half, leap, going_up)

    def hop_x(sorted_, got, send, recv, q, d):
        return remote(
            sorted_.at[q, d], got.at[q, x], send.at[q, d], recv.at[q, d], (z, (x + d) % EXPERTS, t)
        )

    def hop_y(got, fin, send, recv, q, source, gl):
        return remote(
            got.at[q, source, gl], fin, send.at[q, source * 2 + gl], recv.at[q, t], (z, x, source * 2 + gl)
        )

    def ring_start(copy, q):
        copy(q, 0, 0, True).start()
        copy(q, 1, 0, False).start()
        copy(q, 1, 0, True).start()
        copy(q, 0, 0, False).start()

    def ring_forward(copy, q):
        copy(q, 0, 0, True).wait_recv()
        copy(q, 0, 1, True).start()
        copy(q, 1, 0, False).wait_recv()
        copy(q, 1, 1, False).start()

    def ring_finish(copy, q):
        copy(q, 1, 0, True).wait_recv()
        copy(q, 0, 0, False).wait_recv()
        copy(q, 0, 1, True).wait_recv()
        copy(q, 1, 1, False).wait_recv()

    def ring_sent(copy, q):
        for half in range(2):
            copy(q, half, 0, True).wait_send()
            copy(q, half, 0, False).wait_send()
        copy(q, 0, 1, True).wait_send()
        copy(q, 1, 1, False).wait_send()

    def sort(gathered, sorted_, got, q):
        for d in range(EXPERTS):
            to = (x + d) % EXPERTS
            for place in range(OWN):
                p = to * OWN + place
                picks = [sel[p, e] for e in range(WINDOW)]
                for gl in range(GROUPS):
                    shape = gathered.shape[4:]
                    value = None
                    for e in range(WINDOW):
                        part = gathered[q, e // OWN, e % OWN, gl].reshape(-1, 16, BLK) * picks[e][None]
                        value = part if value is None else value + part
                    value = value.reshape(shape)
                    if d == 0:
                        got[q, x, gl, place] = value
                    else:
                        sorted_[q, d, gl, place] = value

    def start_y(got, fin_of, send, recv, q, source):
        for gl in range(GROUPS):
            here = source * 2 + gl == t

            @pl.when(jnp.logical_not(here))
            def _():
                hop_y(got, fin_of(q, t), send, recv, q, source, gl).start()

            @pl.when(here)
            def _():
                fin_of(q, t)[...] = got[q, source, gl]

    def sent_y(got, fin_of, send, recv, q):
        for d in range(1, TENSORS):
            to = (t + d) % TENSORS
            hop_y(got, fin_of(q, t), send, recv, q, to // 2, to % 2).wait_send()

    def got_y(got, fin_of, send, recv, q):
        for d in range(1, TENSORS):
            source = (t + d) % TENSORS
            ref = fin_of(q, source)
            remote(ref, ref, send.at[q, source], recv.at[q, source], (z, x, source)).wait_recv()

    def route(gathered, sorted_, got, fin_of, x_s, x_r, y_s, y_r, q):
        sort(gathered, sorted_, got, q)
        for d in range(1, EXPERTS):
            hop_x(sorted_, got, x_s, x_r, q, d).start()
        start_y(got, fin_of, y_s, y_r, q, x)

    def pass_on(sorted_, got, fin_of, x_s, x_r, y_s, y_r, q):
        for d in range(1, EXPERTS):
            hop_x(sorted_, got, x_s, x_r, q, d).wait_recv()
            start_y(got, fin_of, y_s, y_r, q, (x + EXPERTS - d) % EXPERTS)

    def fin_a_of(q, source):
        return fin_a.at[q, source]

    def fin_b_of(q, source):
        return fin_b.at[q, z, source]

    def c1(d):
        return remote(z_c.at[z], z_c.at[z], c1_s.at[d], c1_r.at[d], ((z + d) % SECTIONS, x, t))

    def c2(d):
        return remote(z_c, x_c.at[x], c2_s.at[d], c2_r.at[d], (z, (x + d) % EXPERTS, t))

    def c3(source, gl):
        to = source * 2 + gl
        return remote(x_c.at[source], fin_c.at[t], c3_s.at[to], c3_r.at[t], (z, x, to))

    def got_c3(source):
        ref = fin_c.at[source]
        return remote(ref, ref, c3_s.at[source], c3_r.at[source], (z, x, source))

    def numbers_along_x():
        for d in range(1, SECTIONS):
            c1(d).wait_recv()
        for d in range(1, EXPERTS):
            c2(d).start()
        x_c[x] = z_c[...]

    def numbers_along_y():
        for d in range(1, EXPERTS):
            c2(d).wait_recv()
        for d in range(1, TENSORS):
            to = (t + d) % TENSORS
            c3(to // 2, to % 2).start()
        fin_c[t] = x_c[t // 2]

    for d in range(1, SECTIONS):
        c1(d).start()

    def begin_b(q, _):
        for d in (2, 1, 3):
            b1(q, d).start()
        slot, row = share_place(z, q)
        row = pl.multiple_of(row, ROWS_B)
        for le in range(OWN):
            for gl in range(GROUPS):
                z_b[q, z, le, gl] = packed[le, gl, slot, pl.ds(row, ROWS_B)]
        return 0

    def begin_a(q, _):
        row = pl.multiple_of(q * ROWS_A, ROWS_A)
        for le in range(OWN):
            for gl in range(GROUPS):
                z_a[q, z, le, gl] = packed[le, gl, pl.ds(0, SLOTS_A), pl.ds(row, ROWS_A)]
        ring_start(a1, q)
        return 0

    lax.fori_loop(0, CHUNKS_B, begin_b, 0)
    if SLOTS_A:
        lax.fori_loop(0, CHUNKS_A, begin_a, 0)

    def keep_rest(i, _):
        le, r = i // ROW_BLOCKS, i % ROW_BLOCKS
        row = pl.multiple_of(r * BLK, BLK)
        limit = count[z * OWN + le]
        for column in range(2 * GROUPS):
            block = r * 2 + column % 2
            sent = 0
            for j in range(KEEP):
                chosen = (kept[le, 0, column // 2, j] == block).astype(jnp.int32)
                sent = sent + chosen * (j < limit).astype(jnp.int32)
            sent = sent.astype(jnp.float32)
            at = (le, pl.ds(row, BLK), pl.ds(column * BLK, BLK))
            change = upd[at].astype(jnp.float32) + res_out[at]
            rounded = change.astype(jnp.bfloat16).astype(jnp.float32)
            res_out[at] = change - sent * rounded
        return 0

    for load in loads:
        load.wait()
    lax.fori_loop(0, OWN * ROW_BLOCKS, keep_rest, 0)
    numbers_along_x()

    route_b = functools.partial(route, z_b, s_b, x_b, fin_b_of, b2_s, b2_r, b3_s, b3_r)
    pass_b = functools.partial(pass_on, s_b, x_b, fin_b_of, b2_s, b2_r, b3_s, b3_r)
    route_a = functools.partial(route, z_a, s_a, x_a, fin_a_of, a2_s, a2_r, a3_s, a3_r)
    pass_a = functools.partial(pass_on, s_a, x_a, fin_a_of, a2_s, a2_r, a3_s, a3_r)

    def b_p1(q):
        for d in range(1, SECTIONS):
            b1(q, d).wait_recv()
        route_b(q)

    def b_p3(q):
        got_y(x_b, fin_b_of, b3_s, b3_r, q)
        ring_start(b4, q)

    def a_p2(q):
        ring_finish(a1, q)
        route_a(q)

    steps = [
        (CHUNKS_B, 0, b_p1),
        (CHUNKS_A if SLOTS_A else 0, 0, lambda q: ring_forward(a1, q)),
        (CHUNKS_B, 1, pass_b),
        (CHUNKS_B, 2, b_p3),
        (CHUNKS_A if SLOTS_A else 0, 1, a_p2),
        (CHUNKS_A if SLOTS_A else 0, 2, pass_a),
        (CHUNKS_B, 4, lambda q: ring_forward(b4, q)),
    ]

    def step(s, _):
        pl.when(s == 1)(numbers_along_y)
        for n, lag, work in steps:
            if n:
                pl.when((s >= lag) & (s < lag + n))(functools.partial(work, s - lag))
        return 0

    lax.fori_loop(0, max(n + lag for n, lag, _ in steps if n), step, 0)

    def end_b(q, _):
        ring_finish(b4, q)
        for d in range(1, SECTIONS):
            b1(q, d).wait_send()
        for d in range(1, EXPERTS):
            hop_x(s_b, x_b, b2_s, b2_r, q, d).wait_send()
        sent_y(x_b, fin_b_of, b3_s, b3_r, q)
        ring_sent(b4, q)
        return 0

    def end_a(q, _):
        got_y(x_a, fin_a_of, a3_s, a3_r, q)
        ring_sent(a1, q)
        for d in range(1, EXPERTS):
            hop_x(s_a, x_a, a2_s, a2_r, q, d).wait_send()
        sent_y(x_a, fin_a_of, a3_s, a3_r, q)
        return 0

    if SLOTS_A:
        lax.fori_loop(0, CHUNKS_A, end_a, 0)
    lax.fori_loop(0, CHUNKS_B, end_b, 0)
    for d in range(1, SECTIONS):
        c1(d).wait_send()
    for d in range(1, EXPERTS):
        c2(d).wait_send()
    for d in range(1, TENSORS):
        to = (t + d) % TENSORS
        got_c3(to).wait_recv()
        c3(to // 2, to % 2).wait_send()
    stage.wait()


def push(packed, numbers, update, residual, kept, count, slots, served):
    bf = jnp.bfloat16
    hbm, smem, vmem = pltpu.HBM, pltpu.SMEM, pltpu.VMEM
    ca, cb = CHUNKS_A, CHUNKS_B
    sa = max(SLOTS_A, 1)
    sems = []
    for chunks, width in ((ca, 6), (ca, 4), (ca, 8), (cb, 4), (cb, 4), (cb, 8), (cb, 6)):
        sems += [pltpu.SemaphoreType.DMA((chunks, width))] * 2
    for width in (4, 4, 8):
        sems += [pltpu.SemaphoreType.DMA((width,))] * 2
    return pl.pallas_call(
        push_kernel,
        out_shape=(
            vmem(residual.shape, jnp.float32),
            vmem(served.shape[1:], bf),
            vmem((ca, TENSORS, OWN, sa, ROWS_A, BLK), bf),
            vmem((cb, SECTIONS, TENSORS, OWN, ROWS_B, BLK), bf),
            vmem((TENSORS, SECTIONS, 1, BLK), jnp.int32),
        ),
        in_specs=[
            pl.BlockSpec(memory_space=vmem),
            pl.BlockSpec(memory_space=vmem),
            pl.BlockSpec(memory_space=hbm),
            pl.BlockSpec(memory_space=hbm),
            pl.BlockSpec(memory_space=smem),
            pl.BlockSpec(memory_space=smem),
            pl.BlockSpec(memory_space=smem),
            pl.BlockSpec(memory_space=hbm),
        ],
        out_specs=(pl.BlockSpec(memory_space=vmem),) * 5,
        scratch_shapes=[
            vmem(update.shape, bf),
            vmem((WINDOW, WINDOW, 16, BLK), bf),
            vmem((ca, SECTIONS, OWN, GROUPS, sa, ROWS_A, BLK), bf),
            vmem((ca, EXPERTS, GROUPS, OWN, sa, ROWS_A, BLK), bf),
            vmem((ca, EXPERTS, GROUPS, OWN, sa, ROWS_A, BLK), bf),
            vmem((cb, SECTIONS, OWN, GROUPS, ROWS_B, BLK), bf),
            vmem((cb, EXPERTS, GROUPS, OWN, ROWS_B, BLK), bf),
            vmem((cb, EXPERTS, GROUPS, OWN, ROWS_B, BLK), bf),
            vmem((SECTIONS, 1, BLK), jnp.int32),
            vmem((EXPERTS, SECTIONS, 1, BLK), jnp.int32),
            pltpu.SemaphoreType.DMA((5,)),
            *sems,
        ],
        compiler_params=pltpu.CompilerParams(
            collective_id=0, has_side_effects=True, vmem_limit_bytes=48 << 20
        ),
        name="push",
    )(packed, numbers, update, residual, kept, count, slots, served)


def apply_kernel(codes, count, slots, staged_in, fin_a, fin_b, out, staged, sem):
    del staged_in
    _, x, t = own_place()

    def region(place, source):
        rows = ROW_BLOCKS * BLK
        at = pl.ds(pl.multiple_of(source * rows, rows), rows)
        return pltpu.make_async_copy(staged.at[place, at], out.at[0, place, at], sem)

    for place in range(OWN):
        p = x * OWN + place
        e = sum(jnp.where(slots[i] == p, i, 0) for i in range(WINDOW))
        limit = count[e]
        base = (e % OWN) * GROUPS * KEEP + (t % GROUPS) * KEEP

        def row_range(source, _):
            for j in range(KEEP):
                code = codes[source, e // OWN, 0, base + j]

                @pl.when(j < limit)
                def _():
                    row = source * (ROW_BLOCKS * BLK) + (code // 2) * BLK
                    column = pl.ds(pl.multiple_of((code % 2) * BLK, BLK), BLK)

                    def add(first, rows, piece):
                        at = (place, pl.ds(pl.multiple_of(row + first, 16), rows), column)
                        total = staged[at].astype(jnp.float32) + piece.astype(jnp.float32)
                        staged[at] = total.astype(jnp.bfloat16)

                    if j < SLOTS_A:
                        for q in range(CHUNKS_A):
                            add(q * ROWS_A, ROWS_A, fin_a[q, source, place, j])
                    else:
                        for section in range(SECTIONS):
                            for q in range(CHUNKS_B):
                                slot, first = share_place(section, q)
                                if slot == j:
                                    add(first, ROWS_B, fin_b[q, section, source, place])

            region(place, source).start()
            return 0

        lax.fori_loop(0, TENSORS, row_range, 0)

    for place in range(OWN):
        for source in range(TENSORS):
            region(place, source).wait()


def apply(codes, count, slots, staged, fin_a, fin_b, served):
    smem, vmem = pltpu.SMEM, pltpu.VMEM
    return pl.pallas_call(
        apply_kernel,
        out_shape=(
            jax.ShapeDtypeStruct(served.shape, served.dtype),
            vmem(staged.shape, staged.dtype),
        ),
        in_specs=[pl.BlockSpec(memory_space=smem)] * 3 + [pl.BlockSpec(memory_space=vmem)] * 3,
        out_specs=(pl.BlockSpec(memory_space=pltpu.HBM), pl.BlockSpec(memory_space=vmem)),
        scratch_shapes=[pltpu.SemaphoreType.DMA],
        input_output_aliases={3: 1},
        compiler_params=pltpu.CompilerParams(vmem_limit_bytes=32 << 20),
        name="apply",
    )(codes, count, slots, staged, fin_a, fin_b)[0]


def on_device(update, residual, kept_blocks, kept_count, serving_slot, served_up):
    packed, numbers = pack(update, residual, kept_blocks)
    res_new, staged, fin_a, fin_b, codes = push(
        packed, numbers, update, residual, kept_blocks, kept_count, serving_slot, served_up
    )
    served_new = apply(codes, kept_count, serving_slot, staged, fin_a, fin_b, served_up)
    return served_new, res_new


def solution(mesh):
    return jax.shard_map(
        on_device,
        mesh=mesh,
        in_specs=(
            P("section", "tensor", "expert"),
            P("section", "tensor", "expert"),
            P("section", "tensor", "expert", None),
            P(),
            P(),
            P("section", "expert", None, "tensor"),
        ),
        out_specs=(P("section", "expert", None, "tensor"), P("section", "tensor", "expert")),
        check_vma=False,
    )
```

time: 317 us -> 59 us (0.19)
  waiting for transfers between devices: 109 us -> 0 us
  local copies, waits for them, and re-layouts: 103 us -> 7.36 us
  matrix products: 50.1 us -> 0 us
  Pallas kernels: 0 us -> 49.8 us
  starting transfers between devices: 26.9 us -> 0 us
  other arithmetic: 26.3 us -> 0 us
    all_to_all x4 -> x0, waiting for transfers between devices: 109 us -> none  [the longest x1 60 us: on_device(): lax.all_to_all(as_sent(copies), ('section', 'expert'), split_axis=0, conc...]
    dot_general x2 -> x0, matrix products: 50.1 us -> none  [the longest x1 41 us: on_device(): jnp.einsum('es,stpabxy->etaxpby', select_slot, grid, preferred_element_ty...]
    pallas_call x0 -> x3, Pallas kernels: none -> 49.8 us  [the longest x1 44.4 us: push(): pl.pallas_call(push_kernel, out_shape=(vmem(residual.shape, jnp.float32),...]
    gather x50 -> x0, local copies, waits for them, and re-layouts: 43.9 us -> none
    all_to_all x4 -> x0, starting transfers between devices: 26.9 us -> none  [the longest x1 8.43 us: on_device(): lax.all_to_all(copy_codes, ('section', 'expert'), split_axis=0, concat_ax...]
    transpose x2 -> x0, local copies, waits for them, and re-layouts: 24.5 us -> none  [the longest x1 24.4 us: on_device(): jnp.einsum('es,stpabxy->etaxpby', select_slot, grid, preferred_element_ty...]
    convert_element_type x1 -> x0, other arithmetic: 17.7 us -> none  [on_device(): weights = (served_up[0].astype(jnp.float32) + by_slot).astype(jnp.bfloat16)]
    convert_element_type x1 -> x0, local copies, waits for them, and re-layouts: 10.8 us -> none  [on_device(): grid = jnp.einsum('stpjb,stpjxy->stpbxy', one_hot, arrived, preferred_ele...]
  transfers between devices with their start and end apart: 4 -> 0, of which waited for: 2 -> 0; matrix products, arithmetic and copies ran while one was open for 19% -> 0% of each run, Pallas kernels for 0% -> 0%
where the time goes in v1:
time: 59 us; the launch traced here: 57.8 us
  Pallas kernels  49.8 us (84%)
  local copies, waits for them, and re-layouts  7.36 us (12%)
  between operations  0.67 us (1%)
    pallas_call x1, Pallas kernels, push(): pl.pallas_call(push_kernel, out_shape=(vmem(residual.shape, jnp.float32),...  44.4 us
    unnamed x15, local copies, waits for them, and re-layouts  7.36 us
    pallas_call x1, Pallas kernels, apply(): pl.pallas_call(apply_kernel, out_shape=(jax.ShapeDtypeStruct(served.shape...  3.92 us
    pallas_call x1, Pallas kernels, pack(): pl.pallas_call(pack_kernel, out_shape=(vmem((OWN, GROUPS, KEEP, BLK, BLK)...  1.51 us

profile of v1, /device:TPU:1, one launch (start us, length us, event | category | flops | bytes accessed | tf_op | source)
XLA Modules:
  0.0 57.8 jit_solution(9824730494502175508)
XLA Ops:
  0.6 0.0 copy-start
  0.6 2.0 %copy-done = f32[2,896,512]{2,1,0:T(8,128)S(1)} copy-done((f32[2,896,512]{2,1,0:T(8,128)S(1)}, f32[2,896,512]{2,1,0:T(8,128)}, u32[]{:S(2)}) %copy-start) | copy-done | bytes 3670040
  2.7 0.0 copy-start.1
  2.7 1.5 %copy-done.1 = bf16[2,896,512]{2,1,0:T(8,128)(2,1)S(1)} copy-done((bf16[2,896,512]{2,1,0:T(8,128)(2,1)S(1)}, bf16[2,896,512]{2,1,0:T(8,128)(2,1)}, u32[]{:S(2)}) %copy-start.1) | copy-done | bytes 1835032
  4.2 0.0 copy-start.3
  4.2 0.7 %copy-done.3 = s32[2,1,2,4]{3,2,1,0:T(2,128)S(1)} copy-done((s32[2,1,2,4]{3,2,1,0:T(2,128)S(1)}, s32[2,1,2,4]{3,2,1,0:T(2,128)}, u32[]{:S(2)}) %copy-start.3) | copy-done | bytes 88
  4.9 1.5 %pack.1 = (bf16[2,2,4,128,128]{4,3,2,1,0:T(8,128)(2,1)S(1)}, s32[1,128]{1,0:T(1,128)S(1)}) custom-call(bf16[2,896,512]{2,1,0:T(8,128)(2,1)S(1)} %copy-done.1, f32[2,896,512]{2,1,0:T(8,128)S(1)} %copy-done, s32[2,1,2,4]{3,2,1,0:T(2,128)S(1)} %copy-done.3), custom_call_target="tpu_custom_call" | custom-call | tf_op jit(solution)/shard_map/pack/pallas_call | solution.py:67
  6.4 0.0 copy-start.2
  6.4 0.8 %copy-done.2 = bf16[2,2,4,128,128]{4,3,2,1,0:T(8,128)(2,1)} copy-done((bf16[2,2,4,128,128]{4,3,2,1,0:T(8,128)(2,1)}, bf16[2,2,4,128,128]{4,3,2,1,0:T(8,128)(2,1)S(1)}, u32[]{:S(2)}) %copy-start.2) | copy-done | bytes 524312
  7.2 0.0 copy-start.6
  7.2 0.5 copy-done.6
  7.7 0.0 copy-start.4
  7.7 0.0 copy-start.5
  7.7 44.4 %push.1 = (f32[2,896,512]{2,1,0:T(8,128)S(1)}, bf16[2,7168,256]{2,1,0:T(8,128)(2,1)S(1)}, bf16[4,8,2,2,32,128]{5,4,3,2,1,0:T(8,128)(2,1)S(1)}, bf16[4,4,8,2,16,1...) custom-call(bf16[2,2,4,128,128]{4,3,2,1,0:T(8,128)(2,1)} %copy-done.2, s32[1,128]{1,0:T(1,128)} %copy-done.6, ...), custom_call_target="tpu_custom_call" | custom-call | tf_op jit(solution)/shard_map/push/pallas_call | solution.py:397
  52.0 1.8 %copy.11 = f32[2,896,512]{2,1,0:T(8,128)} copy(f32[2,896,512]{2,1,0:T(8,128)S(1)} %get-tuple-element.19) | data formatting | bytes 7340032
  53.9 0.0 copy-done.4
  53.9 0.0 copy-done.5
  53.9 3.9 %apply.1 = (bf16[1,2,7168,256]{3,2,1,0:T(8,128)(2,1)}, bf16[2,7168,256]{2,1,0:T(8,128)(2,1)S(1)}) custom-call(s32[8,4,1,128]{3,2,1,0:T(1,128)S(1)} %get-tuple-element.12.codes, s32[8]{0:T(128)S(1)} %copy-done.4, s32[8]{0:T(128)S(1)} %copy-done.5, bf16[2,7168,256]{2,1,0:T(8,128)(2,1)S(1)} %get-tuple-element.13.staged_in, ...), custom_call_target="tpu_custom_call", output_to_operand_aliasing={{1}: (3, {})} | custom-call | tf_op jit(solution)/shard_map/apply/pallas_call | solution.py:489
Async XLA Ops:
  0.6 2.0 %copy-start = (f32[2,896,512]{2,1,0:T(8,128)S(1)}, f32[2,896,512]{2,1,0:T(8,128)}, u32[]{:S(2)}) copy-start(f32[2,896,512]{2,1,0:T(8,128)} %residual.3) | copy-start | bytes 11010052
  2.7 1.5 %copy-start.1 = (bf16[2,896,512]{2,1,0:T(8,128)(2,1)S(1)}, bf16[2,896,512]{2,1,0:T(8,128)(2,1)}, u32[]{:S(2)}) copy-start(bf16[2,896,512]{2,1,0:T(8,128)(2,1)} %update.3) | copy-start | bytes 5505028
  4.2 0.7 %copy-start.3 = (s32[2,1,2,4]{3,2,1,0:T(2,128)S(1)}, s32[2,1,2,4]{3,2,1,0:T(2,128)}, u32[]{:S(2)}) copy-start(s32[2,1,2,4]{3,2,1,0:T(2,128)} %kept.3) | copy-start | bytes 196
  6.4 0.8 %copy-start.2 = (bf16[2,2,4,128,128]{4,3,2,1,0:T(8,128)(2,1)}, bf16[2,2,4,128,128]{4,3,2,1,0:T(8,128)(2,1)S(1)}, u32[]{:S(2)}) copy-start(bf16[2,2,4,128,128]{4,3,2,1,0:T(8,128)(2,1)S(1)} %get-tuple-element.10.packed) | copy-start | bytes 1572868
  7.2 0.5 copy-start.6
  7.7 46.2 %copy-start.4 = (s32[8]{0:T(128)S(1)}, s32[8]{0:T(128)}, u32[]{:S(2)}) copy-start(s32[8]{0:T(128)} %count.3) | copy-start | bytes 100
  7.7 46.2 %copy-start.5 = (s32[8]{0:T(128)S(1)}, s32[8]{0:T(128)}, u32[]{:S(2)}) copy-start(s32[8]{0:T(128)} %slots.3) | copy-start | bytes 100

commit v2 on v0

v2 whole, which is shorter than its diff:
```python
import functools

import jax
import jax.numpy as jnp
from jax import lax
from jax.experimental import pallas as pl
from jax.experimental.pallas import tpu as pltpu
from jax.sharding import PartitionSpec as P

MESH = pl.DeviceIdType.MESH
BLK = 128
SECTIONS = 4
EXPERTS = 4
TENSORS = 8
OWN = 2
GROUPS = 2
KEEP = 4
ROW_BLOCKS = 7
WINDOW = 8
SLOTS_A = 1
CHUNKS_A = 2
CHUNKS_B = 6
ROWS_A = BLK // CHUNKS_A
SHARE_B = (KEEP - SLOTS_A) * BLK // SECTIONS
ROWS_B = SHARE_B // CHUNKS_B


SCHEDULE = (
    "c", "b0", "b1", "b2", "b3", "b4", "b5", "a0", "a1", "l", "br0", "br1",
    "cr", "br2", "br3", "br4", "br5", "k", "af0", "bs0", "af1", "bs1", "ar0", "bs2",
    "bf0", "bs3", "ar1", "bs4", "bf1", "bf2", "bs5", "be0", "bf3", "bf4", "be1", "be2",
    "ae0", "bf5", "be3", "be4", "be5", "ae1", "ce",
)


def own_place():
    return lax.axis_index("section"), lax.axis_index("expert"), lax.axis_index("tensor")


def share_place(section, chunk):
    first = section * SHARE_B + chunk * ROWS_B
    return SLOTS_A + first // BLK, first % BLK


def push_kernel(
    update, residual, kept, count, slots, served,
    res_out, staged, fin_a, fin_b, fin_c,
    upd_0, upd_1, rest_0, rest_1, packed, sel, z_a, s_a, z_b, s_b, z_c,
    load_sem, stage_sem, a_send, a_up, a_down, a_far, a_got, b_send, b_in, b_got, b_up, b_down, b_far,
    c_send, c_in, c_got,
):
    z, x, t = own_place()
    up, down = ((z + 1) % SECTIONS, x, t), ((z + 3) % SECTIONS, x, t)
    on_diagonal = t // GROUPS == x

    upd, rest = (upd_0, upd_1), (rest_0, rest_1)
    loads = [[] for _ in range(OWN)]
    for le in range(OWN):
        for column in range(2 * GROUPS):
            lanes = pl.ds(column * BLK, BLK)
            for n, (src, dst) in enumerate(((update, upd[le]), (residual, rest[le]))):
                dst = dst.at[column // 2, pl.ds(column % 2 * ROW_BLOCKS, ROW_BLOCKS)]
                loads[le].append(
                    pltpu.make_async_copy(src.at[le, :, :, lanes], dst, load_sem.at[le, 2 * column + n])
                )
    stage = pltpu.make_async_copy(served.at[0], staged, stage_sem)
    for load in (*loads[0], *loads[1]):
        load.start()

    barrier = pltpu.get_barrier_semaphore()
    for d in range(1, SECTIONS):
        pl.semaphore_signal(barrier, inc=1, device_id=((z + d) % SECTIONS, x, t), device_id_type=MESH)
    for d in range(TENSORS):
        to = (t + d) % TENSORS

        def greet(to=to):
            pl.semaphore_signal(barrier, inc=1, device_id=(z, t // GROUPS, to), device_id_type=MESH)

        if d == 0:
            pl.when(jnp.logical_not(on_diagonal))(greet)
        else:
            greet()

    for p in range(WINDOW):
        for e in range(WINDOW):
            here = (slots[e] == p).astype(jnp.float32)
            sel[p, e] = jnp.full(sel.shape[2:], here, jnp.float32).astype(sel.dtype)
    lanes = lax.broadcasted_iota(jnp.int32, (1, BLK), 1)
    numbers = jnp.zeros((1, BLK), jnp.int32)
    for i in range(OWN * GROUPS * KEEP):
        number = kept[i // (GROUPS * KEEP), 0, i // KEEP % GROUPS, i % KEEP]
        numbers = numbers + number * (lanes == i).astype(jnp.int32)
    z_c[z] = numbers

    for le in range(OWN):
        for load in loads[le]:
            load.wait()
        for gl in range(GROUPS):
            for j in range(KEEP):
                number = kept[le, 0, gl, j]
                at = (gl, (number & 1) * ROW_BLOCKS + (number >> 1))
                change = upd[le][at].astype(jnp.float32) + rest[le][at]
                packed[le, gl, j] = change.astype(jnp.bfloat16)
    pl.semaphore_wait(barrier, SECTIONS - 1 + TENSORS - on_diagonal.astype(jnp.int32))

    def remote(src, dst, send, recv, to):
        return pltpu.make_async_remote_copy(
            src_ref=src, dst_ref=dst, send_sem=send, recv_sem=recv, device_id=to, device_id_type=MESH
        )

    def wait_for(ref, sem):
        pltpu.make_async_copy(ref, ref, sem).wait()

    def across(src_of, dst, send, got):
        for d in range(EXPERTS):
            for gl in range(GROUPS):
                to = x * GROUPS + gl
                src = src_of(d, gl)
                copy = remote(src, dst, send, got, (z, (x + d) % EXPERTS, to))
                if d:
                    copy.start()
                else:
                    own = pltpu.make_async_copy(src, dst, got)
                    pl.when(to != t)(copy.start)
                    pl.when(to == t)(own.start)

    def across_sent(whole, send):
        n = whole.shape[0]

        @pl.when(on_diagonal)
        def _():
            wait_for(whole.at[pl.ds(0, n - n // TENSORS)], send)

        @pl.when(jnp.logical_not(on_diagonal))
        def _():
            wait_for(whole, send)

    def sort(gathered, sorted_, q):
        for d in range(EXPERTS):
            for place in range(OWN):
                p = (x + d) % EXPERTS * OWN + place
                picks = [sel[p, e] for e in range(WINDOW)]
                for gl in range(GROUPS):
                    value = None
                    for e in range(WINDOW):
                        part = gathered[q, e // OWN, e % OWN, gl].reshape(-1, 16, BLK) * picks[e][None]
                        value = part if value is None else value + part
                    sorted_[q, d, gl, place] = value.reshape(gathered.shape[4:])

    def ring_start(buffer, q, send, go_up, go_down):
        ref = buffer.at[q, z]
        remote(ref, ref, send, go_up.at[q], up).start()
        remote(ref, ref, send, go_down.at[q], down).start()

    def ring_forward(buffer, q, send, go_up, go_down, far):
        if q % 2 == 0:
            ref = buffer.at[q, (z + 3) % SECTIONS]
            wait_for(ref, go_up.at[q])
            remote(ref, ref, send, far.at[q], up).start()
        else:
            ref = buffer.at[q, (z + 1) % SECTIONS]
            wait_for(ref, go_down.at[q])
            remote(ref, ref, send, far.at[q], down).start()

    def ring_finish(buffer, q, go_up, go_down, far):
        ref = buffer.at[q, z]
        wait_for(ref, (go_down if q % 2 == 0 else go_up).at[q])
        wait_for(ref, far.at[q])

    def share_of(section, q):
        slot, row = share_place(section, q)
        return packed.at[:, :, slot, pl.ds(pl.multiple_of(row, ROWS_B), ROWS_B)]

    def b_begin(q):
        for d in (2, 1, 3):
            to = (z + d) % SECTIONS
            remote(share_of(to, q), z_b.at[q, z], b_send.at[0, q], b_in.at[q], (to, x, t)).start()
        z_b[q, z] = share_of(z, q)[...]

    def b_route(q):
        wait_for(z_b.at[q, pl.ds(0, SECTIONS - 1)], b_in.at[q])
        sort(z_b, s_b, q)
        across(lambda d, gl: s_b.at[q, d, gl], fin_b.at[q, z, t], b_send.at[1, q], b_got.at[q])

    def b_spread(q):
        wait_for(fin_b.at[q, z], b_got.at[q])
        ring_start(fin_b, q, b_send.at[2, q], b_up, b_down)

    def b_forward(q):
        ring_forward(fin_b, q, b_send.at[2, q], b_up, b_down, b_far)

    def b_finish(q):
        ring_finish(fin_b, q, b_up, b_down, b_far)

    def a_begin(q):
        z_a[q, z] = packed[:, :, pl.ds(0, SLOTS_A), pl.ds(q * ROWS_A, ROWS_A)]
        ring_start(z_a, q, a_send.at[0, q], a_up, a_down)

    def a_forward(q):
        ring_forward(z_a, q, a_send.at[0, q], a_up, a_down, a_far)

    def a_route(q):
        ring_finish(z_a, q, a_up, a_down, a_far)
        sort(z_a, s_a, q)
        across(lambda d, gl: s_a.at[q, d, gl], fin_a.at[q, t], a_send.at[1, q], a_got.at[q])

    def a_finish(q):
        wait_for(fin_a.at[q], a_got.at[q])

    def c_begin(_):
        for d in range(1, SECTIONS):
            remote(z_c.at[z], z_c.at[z], c_send.at[0], c_in, ((z + d) % SECTIONS, x, t)).start()

    def c_route(_):
        wait_for(z_c.at[pl.ds(0, SECTIONS - 1)], c_in)
        across(lambda d, gl: z_c, fin_c.at[t], c_send.at[1], c_got)

    def c_finish(_):
        wait_for(fin_c, c_got)

    def load_served(_):
        stage.start()

    def keep_rest(_):
        for le in range(OWN):
            limit = count[z * OWN + le]

            def row_block(r, _, le=le, limit=limit):
                row = pl.ds(pl.multiple_of(r * BLK, BLK), BLK)
                for column in range(2 * GROUPS):
                    block = r * 2 + column % 2
                    sent = 0
                    for j in range(KEEP):
                        chosen = (kept[le, 0, column // 2, j] == block).astype(jnp.int32)
                        sent = sent + chosen * (j < limit).astype(jnp.int32)
                    sent = sent.astype(jnp.float32)
                    at = (column // 2, column % 2 * ROW_BLOCKS + r)
                    change = upd[le][at].astype(jnp.float32) + rest[le][at]
                    rounded = change.astype(jnp.bfloat16).astype(jnp.float32)
                    res_out[le, row, pl.ds(column * BLK, BLK)] = change - sent * rounded
                return 0

            lax.fori_loop(0, ROW_BLOCKS, row_block, 0)

    work = {
        "b": b_begin, "br": b_route, "bs": b_spread, "bf": b_forward, "be": b_finish,
        "a": a_begin, "af": a_forward, "ar": a_route, "ae": a_finish,
        "c": c_begin, "cr": c_route, "ce": c_finish, "k": keep_rest, "l": load_served,
    }
    for item in SCHEDULE:
        name = item.rstrip("0123456789")
        work[name](int(item[len(name) :] or 0))

    for q in range(CHUNKS_B):
        wait_for(z_b.at[q, pl.ds(0, SECTIONS - 1)], b_send.at[0, q])
        across_sent(fin_b.at[q, z], b_send.at[1, q])
        wait_for(fin_b.at[q, pl.ds(0, 3)], b_send.at[2, q])
    for q in range(CHUNKS_A):
        wait_for(z_a.at[q, pl.ds(0, 3)], a_send.at[0, q])
        across_sent(fin_a.at[q], a_send.at[1, q])
    wait_for(z_c.at[pl.ds(0, SECTIONS - 1)], c_send.at[0])
    across_sent(fin_c, c_send.at[1])
    stage.wait()


def by_rows(array):
    return array.reshape(OWN, ROW_BLOCKS, BLK, array.shape[-1])


def push(update, residual, kept, count, slots, served):
    bf = jnp.bfloat16
    hbm, smem, vmem = pltpu.HBM, pltpu.SMEM, pltpu.VMEM
    ca, cb = CHUNKS_A, CHUNKS_B
    dma = pltpu.SemaphoreType.DMA
    return pl.pallas_call(
        push_kernel,
        out_shape=(
            vmem(residual.shape, jnp.float32),
            vmem(served.shape[1:], bf),
            vmem((ca, TENSORS, OWN, SLOTS_A, ROWS_A, BLK), bf),
            vmem((cb, SECTIONS, TENSORS, OWN, ROWS_B, BLK), bf),
            vmem((TENSORS, SECTIONS, 1, BLK), jnp.int32),
        ),
        in_specs=[pl.BlockSpec(memory_space=m) for m in (hbm, hbm, smem, smem, smem, hbm)],
        out_specs=(pl.BlockSpec(memory_space=vmem),) * 5,
        scratch_shapes=[
            *[vmem((GROUPS, 2 * ROW_BLOCKS, BLK, BLK), bf)] * OWN,
            *[vmem((GROUPS, 2 * ROW_BLOCKS, BLK, BLK), jnp.float32)] * OWN,
            vmem((OWN, GROUPS, KEEP, BLK, BLK), bf),
            vmem((WINDOW, WINDOW, 16, BLK), bf),
            vmem((ca, SECTIONS, OWN, GROUPS, SLOTS_A, ROWS_A, BLK), bf),
            vmem((ca, EXPERTS, GROUPS, OWN, SLOTS_A, ROWS_A, BLK), bf),
            vmem((cb, SECTIONS, OWN, GROUPS, ROWS_B, BLK), bf),
            vmem((cb, EXPERTS, GROUPS, OWN, ROWS_B, BLK), bf),
            vmem((SECTIONS, 1, BLK), jnp.int32),
            dma((OWN, 4 * GROUPS)),
            dma,
            *[dma((2, ca)), dma((ca,)), dma((ca,)), dma((ca,)), dma((ca,))],
            *[dma((3, cb)), dma((cb,)), dma((cb,)), dma((cb,)), dma((cb,)), dma((cb,))],
            *[dma((2,)), dma, dma],
        ],
        compiler_params=pltpu.CompilerParams(
            collective_id=0, has_side_effects=True, vmem_limit_bytes=45 << 20
        ),
        name="push",
    )(by_rows(update), by_rows(residual), kept, count, slots, served)


def apply_kernel(codes, count, slots, rest, staged_in, fin_a, fin_b, out, rest_out, staged, sem, rest_sem):
    del staged_in
    rest_copy = pltpu.make_async_copy(rest, rest_out, rest_sem)
    rest_copy.start()
    _, x, t = own_place()

    def region(place, source):
        rows = ROW_BLOCKS * BLK
        at = pl.ds(pl.multiple_of(source * rows, rows), rows)
        return pltpu.make_async_copy(staged.at[place, at], out.at[0, place, at], sem)

    for place in range(OWN):
        p = x * OWN + place
        e = sum(jnp.where(slots[i] == p, i, 0) for i in range(WINDOW))
        limit = count[e]
        base = (e % OWN) * GROUPS * KEEP + (t % GROUPS) * KEEP

        def row_range(source, _):
            for j in range(KEEP):
                code = codes[source, e // OWN, 0, base + j]

                @pl.when(j < limit)
                def _():
                    row = source * (ROW_BLOCKS * BLK) + (code // 2) * BLK
                    column = pl.ds(pl.multiple_of((code % 2) * BLK, BLK), BLK)

                    def add(first, rows, piece):
                        at = (place, pl.ds(pl.multiple_of(row + first, 16), rows), column)
                        total = staged[at].astype(jnp.float32) + piece.astype(jnp.float32)
                        staged[at] = total.astype(jnp.bfloat16)

                    if j < SLOTS_A:
                        for q in range(CHUNKS_A):
                            add(q * ROWS_A, ROWS_A, fin_a[q, source, place, j])
                    else:
                        for section in range(SECTIONS):
                            for q in range(CHUNKS_B):
                                slot, first = share_place(section, q)
                                if slot == j:
                                    add(first, ROWS_B, fin_b[q, section, source, place])

            region(place, source).start()
            return 0

        lax.fori_loop(0, TENSORS, row_range, 0)

    for place in range(OWN):
        for source in range(TENSORS):
            region(place, source).wait()
    rest_copy.wait()


def apply(codes, count, slots, rest, staged, fin_a, fin_b, served):
    smem, vmem = pltpu.SMEM, pltpu.VMEM
    return pl.pallas_call(
        apply_kernel,
        out_shape=(
            jax.ShapeDtypeStruct(served.shape, served.dtype),
            jax.ShapeDtypeStruct(rest.shape, rest.dtype),
            vmem(staged.shape, staged.dtype),
        ),
        in_specs=[pl.BlockSpec(memory_space=smem)] * 3 + [pl.BlockSpec(memory_space=vmem)] * 4,
        out_specs=[pl.BlockSpec(memory_space=m) for m in (pltpu.HBM, pltpu.HBM, vmem)],
        scratch_shapes=[pltpu.SemaphoreType.DMA] * 2,
        input_output_aliases={4: 2},
        compiler_params=pltpu.CompilerParams(vmem_limit_bytes=32 << 20),
        name="apply",
    )(codes, count, slots, rest, staged, fin_a, fin_b)[:2]


def on_device(update, residual, kept_blocks, kept_count, serving_slot, served_up):
    res_new, staged, fin_a, fin_b, codes = push(
        update, residual, kept_blocks, kept_count, serving_slot, served_up
    )
    return apply(codes, kept_count, serving_slot, res_new, staged, fin_a, fin_b, served_up)


def solution(mesh):
    return jax.shard_map(
        on_device,
        mesh=mesh,
        in_specs=(
            P("section", "tensor", "expert"),
            P("section", "tensor", "expert"),
            P("section", "tensor", "expert", None),
            P(),
            P(),
            P("section", "expert", None, "tensor"),
        ),
        out_specs=(P("section", "expert", None, "tensor"), P("section", "tensor", "expert")),
        check_vma=False,
    )
```

time: 317 us -> 39 us (0.12)
  the two profiles are of different devices: /device:TPU:1 before, /device:TPU:6 now
where the time goes in v2:
time: 39 us; the launch traced here: 38.9 us
  Pallas kernels  38.2 us (98%)
  between operations  0.67 us (2%)
    pallas_call x1, Pallas kernels, push(): pl.pallas_call(push_kernel, out_shape=(vmem(residual.shape, jnp.float32),...  33.3 us
    pallas_call x1, Pallas kernels, apply(): pl.pallas_call(apply_kernel, out_shape=(jax.ShapeDtypeStruct(served.shape...  4.9 us

profile of v2, /device:TPU:6, one launch (start us, length us, event | category | flops | bytes accessed | tf_op | source)
XLA Modules:
  0.0 38.9 jit_solution(3641621644022165335)
XLA Ops:
  0.6 0.0 copy-start
  0.6 0.0 copy-start.1
  0.7 33.3 %push.1 = (f32[2,896,512]{2,1,0:T(8,128)S(1)}, bf16[2,7168,256]{2,1,0:T(8,128)(2,1)S(1)}, bf16[2,8,2,1,64,128]{5,4,3,2,1,0:T(8,128)(2,1)S(1)}, bf16[6,4,8,2,16,1...) custom-call(bf16[2,7,128,512]{3,2,1,0:T(8,128)(2,1)} %bitcast.3, f32[2,7,128,512]{3,2,1,0:T(8,128)} %bitcast.2, ...), custom_call_target="tpu_custom_call" | custom-call | tf_op jit(solution)/shard_map/push/pallas_call | solution.py:275
  33.9 0.0 copy-done
  34.0 0.0 copy-done.1
  34.0 4.9 %apply.1 = (bf16[1,2,7168,256]{3,2,1,0:T(8,128)(2,1)}, f32[2,896,512]{2,1,0:T(8,128)}, bf16[2,7168,256]{2,1,0:T(8,128)(2,1)S(1)}) custom-call(s32[8,4,1,128]{3,2,1,0:T(1,128)S(1)} %get-tuple-element.9.codes, s32[8]{0:T(128)S(1)} %copy-done, s32[8]{0:T(128)S(1)} %copy-done.1, ...), custom_call_target="tpu_custom_call", output_to_operand_aliasing={{2}: (4, {})} | custom-call | tf_op jit(solution)/shard_map/apply/pallas_call | solution.py:363
Async XLA Ops:
  0.6 33.3 %copy-start = (s32[8]{0:T(128)S(1)}, s32[8]{0:T(128)}, u32[]{:S(2)}) copy-start(s32[8]{0:T(128)} %count.3) | copy-start | bytes 100
  0.6 33.3 %copy-start.1 = (s32[8]{0:T(128)S(1)}, s32[8]{0:T(128)}, u32[]{:S(2)}) copy-start(s32[8]{0:T(128)} %slots.3) | copy-start | bytes 100

commit v3 on v2

--- a/solution.py
+++ b/solution.py
@@ -25,11 +25,13 @@
 ROWS_B = SHARE_B // CHUNKS_B
 
 
+DIRECT_B = (5,)
+
 SCHEDULE = (
     "c", "b0", "b1", "b2", "b3", "b4", "b5", "a0", "a1", "l", "br0", "br1",
-    "cr", "br2", "br3", "br4", "br5", "k", "af0", "bs0", "af1", "bs1", "ar0", "bs2",
-    "bf0", "bs3", "ar1", "bs4", "bf1", "bf2", "bs5", "be0", "bf3", "bf4", "be1", "be2",
-    "ae0", "bf5", "be3", "be4", "be5", "ae1", "ce",
+    "br2", "br3", "br4", "br5", "cr", "k", "af0", "bs0", "af1", "bs1", "ar0", "bs2",
+    "bf0", "bs3", "ar1", "bs4", "bf1", "bs5", "bf2", "be0", "bf3", "bf4", "be1", "be2",
+    "ae0", "be3", "be4", "be5", "ae1", "ce",
 )
 
 
@@ -52,6 +54,20 @@
     z, x, t = own_place()
     up, down = ((z + 1) % SECTIONS, x, t), ((z + 3) % SECTIONS, x, t)
     on_diagonal = t // GROUPS == x
+
+    barrier = pltpu.get_barrier_semaphore()
+    for d in range(1, SECTIONS):
+        pl.semaphore_signal(barrier, inc=1, device_id=((z + d) % SECTIONS, x, t), device_id_type=MESH)
+    for d in range(TENSORS):
+        to = (t + d) % TENSORS
+
+        def greet(to=to):
+            pl.semaphore_signal(barrier, inc=1, device_id=(z, t // GROUPS, to), device_id_type=MESH)
+
+        if d == 0:
+            pl.when(jnp.logical_not(on_diagonal))(greet)
+        else:
+            greet()
 
     upd, rest = (upd_0, upd_1), (rest_0, rest_1)
     loads = [[] for _ in range(OWN)]
@@ -67,20 +83,6 @@
     for load in (*loads[0], *loads[1]):
         load.start()
 
-    barrier = pltpu.get_barrier_semaphore()
-    for d in range(1, SECTIONS):
-        pl.semaphore_signal(barrier, inc=1, device_id=((z + d) % SECTIONS, x, t), device_id_type=MESH)
-    for d in range(TENSORS):
-        to = (t + d) % TENSORS
-
-        def greet(to=to):
-            pl.semaphore_signal(barrier, inc=1, device_id=(z, t // GROUPS, to), device_id_type=MESH)
-
-        if d == 0:
-            pl.when(jnp.logical_not(on_diagonal))(greet)
-        else:
-            greet()
-
     for p in range(WINDOW):
         for e in range(WINDOW):
             here = (slots[e] == p).astype(jnp.float32)
@@ -147,24 +149,25 @@
                         value = part if value is None else value + part
                     sorted_[q, d, gl, place] = value.reshape(gathered.shape[4:])
 
-    def ring_start(buffer, q, send, go_up, go_down):
+    def ring_start(buffer, q, send, go_up, go_down, far=None):
         ref = buffer.at[q, z]
         remote(ref, ref, send, go_up.at[q], up).start()
         remote(ref, ref, send, go_down.at[q], down).start()
+        if far is not None:
+            remote(ref, ref, send, far.at[q], ((z + 2) % SECTIONS, x, t)).start()
 
     def ring_forward(buffer, q, send, go_up, go_down, far):
-        if q % 2 == 0:
-            ref = buffer.at[q, (z + 3) % SECTIONS]
+        n = buffer.shape[2] // 2
+        for half, source, got, to in ((0, (z + 3) % SECTIONS, go_up, up), (1, (z + 1) % SECTIONS, go_down, down)):
+            wait_for(buffer.at[q, source], got.at[q])
+            ref = buffer.at[q, source, pl.ds(half * n, n)]
+            remote(ref, ref, send, far.at[q], to).start()
+
+    def ring_finish(buffer, q, go_up, go_down, far, direct=False):
+        ref = buffer.at[q, z]
+        if direct:
             wait_for(ref, go_up.at[q])
-            remote(ref, ref, send, far.at[q], up).start()
-        else:
-            ref = buffer.at[q, (z + 1) % SECTIONS]
             wait_for(ref, go_down.at[q])
-            remote(ref, ref, send, far.at[q], down).start()
-
-    def ring_finish(buffer, q, go_up, go_down, far):
-        ref = buffer.at[q, z]
-        wait_for(ref, (go_down if q % 2 == 0 else go_up).at[q])
         wait_for(ref, far.at[q])
 
     def share_of(section, q):
@@ -184,13 +187,13 @@
 
     def b_spread(q):
         wait_for(fin_b.at[q, z], b_got.at[q])
-        ring_start(fin_b, q, b_send.at[2, q], b_up, b_down)
+        ring_start(fin_b, q, b_send.at[2, q], b_up, b_down, b_far if q in DIRECT_B else None)
 
     def b_forward(q):
         ring_forward(fin_b, q, b_send.at[2, q], b_up, b_down, b_far)
 
     def b_finish(q):
-        ring_finish(fin_b, q, b_up, b_down, b_far)
+        ring_finish(fin_b, q, b_up, b_down, b_far, q in DIRECT_B)
 
     def a_begin(q):
         z_a[q, z] = packed[:, :, pl.ds(0, SLOTS_A), pl.ds(q * ROWS_A, ROWS_A)]

time: 39 us -> 38.1 us (0.977)
  the two profiles are of different devices: /device:TPU:6 before, /device:TPU:1 now
where the time goes in v3:
time: 38.1 us; the launch traced here: 38 us
  Pallas kernels  37.3 us (98%)
  between operations  0.67 us (2%)
    pallas_call x1, Pallas kernels, push(): pl.pallas_call(push_kernel, out_shape=(vmem(residual.shape, jnp.float32),...  32.4 us
    pallas_call x1, Pallas kernels, apply(): pl.pallas_call(apply_kernel, out_shape=(jax.ShapeDtypeStruct(served.shape...  4.9 us

profile of v3, /device:TPU:1, one launch (start us, length us, event | category | flops | bytes accessed | tf_op | source)
XLA Modules:
  0.0 38.0 jit_solution(3184804390126745606)
XLA Ops:
  0.6 0.0 copy-start
  0.6 0.0 copy-start.1
  0.7 32.4 %push.1 = (f32[2,896,512]{2,1,0:T(8,128)S(1)}, bf16[2,7168,256]{2,1,0:T(8,128)(2,1)S(1)}, bf16[2,8,2,1,64,128]{5,4,3,2,1,0:T(8,128)(2,1)S(1)}, bf16[6,4,8,2,16,1...) custom-call(bf16[2,7,128,512]{3,2,1,0:T(8,128)(2,1)} %bitcast.3, f32[2,7,128,512]{3,2,1,0:T(8,128)} %bitcast.2, ...), custom_call_target="tpu_custom_call" | custom-call | tf_op jit(solution)/shard_map/push/pallas_call | solution.py:278
  33.1 0.0 copy-done
  33.1 0.0 copy-done.1
  33.1 4.9 %apply.1 = (bf16[1,2,7168,256]{3,2,1,0:T(8,128)(2,1)}, f32[2,896,512]{2,1,0:T(8,128)}, bf16[2,7168,256]{2,1,0:T(8,128)(2,1)S(1)}) custom-call(s32[8,4,1,128]{3,2,1,0:T(1,128)S(1)} %get-tuple-element.9.codes, s32[8]{0:T(128)S(1)} %copy-done, s32[8]{0:T(128)S(1)} %copy-done.1, ...), custom_call_target="tpu_custom_call", output_to_operand_aliasing={{2}: (4, {})} | custom-call | tf_op jit(solution)/shard_map/apply/pallas_call | solution.py:366
Async XLA Ops:
  0.6 32.5 %copy-start = (s32[8]{0:T(128)S(1)}, s32[8]{0:T(128)}, u32[]{:S(2)}) copy-start(s32[8]{0:T(128)} %count.3) | copy-start | bytes 100
  0.6 32.5 %copy-start.1 = (s32[8]{0:T(128)S(1)}, s32[8]{0:T(128)}, u32[]{:S(2)}) copy-start(s32[8]{0:T(128)} %slots.3) | copy-start | bytes 100

commit v4 on v3

--- a/solution.py
+++ b/solution.py
@@ -18,20 +18,18 @@
 ROW_BLOCKS = 7
 WINDOW = 8
 SLOTS_A = 1
-CHUNKS_A = 2
-CHUNKS_B = 6
+CHUNKS_A = 1
+CHUNKS_B = 3
 ROWS_A = BLK // CHUNKS_A
 SHARE_B = (KEEP - SLOTS_A) * BLK // SECTIONS
 ROWS_B = SHARE_B // CHUNKS_B
 
 
-DIRECT_B = (5,)
-
 SCHEDULE = (
-    "c", "b0", "b1", "b2", "b3", "b4", "b5", "a0", "a1", "l", "br0", "br1",
-    "br2", "br3", "br4", "br5", "cr", "k", "af0", "bs0", "af1", "bs1", "ar0", "bs2",
-    "bf0", "bs3", "ar1", "bs4", "bf1", "bs5", "bf2", "be0", "bf3", "bf4", "be1", "be2",
-    "ae0", "be3", "be4", "be5", "ae1", "ce",
+    "c", "b0", "b3", "b1", "b4", "b2", "b5", "a0", "a1", "l", "br0", "br3",
+    "br1", "br4", "br2", "br5", "cr", "k", "af0", "bs0", "bs3", "af1", "bs1", "bs4",
+    "ar0", "bs2", "bs5", "bf0", "bf3", "ar1", "bf1", "bf4", "bf2", "bf5", "be0", "be3",
+    "be1", "be4", "be2", "be5", "ae0", "ae1", "ce",
 )
 
 
@@ -48,7 +46,7 @@
     update, residual, kept, count, slots, served,
     res_out, staged, fin_a, fin_b, fin_c,
     upd_0, upd_1, rest_0, rest_1, packed, sel, z_a, s_a, z_b, s_b, z_c,
-    load_sem, stage_sem, a_send, a_up, a_down, a_far, a_got, b_send, b_in, b_got, b_up, b_down, b_far,
+    load_sem, stage_sem, a_send, a_up, a_down, a_far, a_got, b_send, b_ring, b_in, b_got, b_up, b_down, b_far,
     c_send, c_in, c_got,
 ):
     z, x, t = own_place()
@@ -113,48 +111,46 @@
     def wait_for(ref, sem):
         pltpu.make_async_copy(ref, ref, sem).wait()
 
-    def across(src_of, dst, send, got):
+    def across(src_of, dst, send, got, gl):
+        to = x * GROUPS + gl
         for d in range(EXPERTS):
-            for gl in range(GROUPS):
-                to = x * GROUPS + gl
-                src = src_of(d, gl)
-                copy = remote(src, dst, send, got, (z, (x + d) % EXPERTS, to))
-                if d:
-                    copy.start()
-                else:
-                    own = pltpu.make_async_copy(src, dst, got)
-                    pl.when(to != t)(copy.start)
-                    pl.when(to == t)(own.start)
-
-    def across_sent(whole, send):
-        n = whole.shape[0]
-
-        @pl.when(on_diagonal)
-        def _():
-            wait_for(whole.at[pl.ds(0, n - n // TENSORS)], send)
-
-        @pl.when(jnp.logical_not(on_diagonal))
-        def _():
-            wait_for(whole, send)
+            src = src_of(d)
+            copy = remote(src, dst, send, got, (z, (x + d) % EXPERTS, to))
+            if d:
+                copy.start()
+            else:
+                own = pltpu.make_async_copy(src, dst, got)
+                pl.when(to != t)(copy.start)
+                pl.when(to == t)(own.start)
+
+    def across_sent(whole, send, gl):
+        to = x * GROUPS + gl
+
+        @pl.when(to == t)
+        def _():
+            wait_for(whole.at[pl.ds(0, EXPERTS - 1)], send)
+
+        @pl.when(to != t)
+        def _():
+            wait_for(whole.at[pl.ds(0, EXPERTS)], send)
+
+    def on_core(gl):
+        return pl.when(t % GROUPS == gl)
 
     def sort(gathered, sorted_, q):
         for d in range(EXPERTS):
             for place in range(OWN):
                 p = (x + d) % EXPERTS * OWN + place
-                picks = [sel[p, e] for e in range(WINDOW)]
-                for gl in range(GROUPS):
-                    value = None
-                    for e in range(WINDOW):
-                        part = gathered[q, e // OWN, e % OWN, gl].reshape(-1, 16, BLK) * picks[e][None]
-                        value = part if value is None else value + part
-                    sorted_[q, d, gl, place] = value.reshape(gathered.shape[4:])
-
-    def ring_start(buffer, q, send, go_up, go_down, far=None):
+                value = None
+                for e in range(WINDOW):
+                    part = gathered[q, e // OWN, e % OWN].reshape(-1, 16, BLK) * sel[p, e][None]
+                    value = part if value is None else value + part
+                sorted_[q, d, place] = value.reshape(gathered.shape[3:])
+
+    def ring_start(buffer, q, send, go_up, go_down):
         ref = buffer.at[q, z]
         remote(ref, ref, send, go_up.at[q], up).start()
         remote(ref, ref, send, go_down.at[q], down).start()
-        if far is not None:
-            remote(ref, ref, send, far.at[q], ((z + 2) % SECTIONS, x, t)).start()
 
     def ring_forward(buffer, q, send, go_up, go_down, far):
         n = buffer.shape[2] // 2
@@ -163,16 +159,12 @@
             ref = buffer.at[q, source, pl.ds(half * n, n)]
             remote(ref, ref, send, far.at[q], to).start()
 
-    def ring_finish(buffer, q, go_up, go_down, far, direct=False):
-        ref = buffer.at[q, z]
-        if direct:
-            wait_for(ref, go_up.at[q])
-            wait_for(ref, go_down.at[q])
-        wait_for(ref, far.at[q])
+    def ring_finish(buffer, q, far):
+        wait_for(buffer.at[q, z], far.at[q])
 
     def share_of(section, q):
-        slot, row = share_place(section, q)
-        return packed.at[:, :, slot, pl.ds(pl.multiple_of(row, ROWS_B), ROWS_B)]
+        slot, row = share_place(section, q % CHUNKS_B)
+        return packed.at[:, q // CHUNKS_B, slot, pl.ds(pl.multiple_of(row, ROWS_B), ROWS_B)]
 
     def b_begin(q):
         for d in (2, 1, 3):
@@ -181,34 +173,53 @@
         z_b[q, z] = share_of(z, q)[...]
 
     def b_route(q):
+        gl, i = q // CHUNKS_B, q % CHUNKS_B
         wait_for(z_b.at[q, pl.ds(0, SECTIONS - 1)], b_in.at[q])
         sort(z_b, s_b, q)
-        across(lambda d, gl: s_b.at[q, d, gl], fin_b.at[q, z, t], b_send.at[1, q], b_got.at[q])
+        across(lambda d: s_b.at[q, d], fin_b.at[i, z, t], b_send.at[1, q], b_got.at[i], gl)
 
     def b_spread(q):
-        wait_for(fin_b.at[q, z], b_got.at[q])
-        ring_start(fin_b, q, b_send.at[2, q], b_up, b_down, b_far if q in DIRECT_B else None)
+        gl, i = q // CHUNKS_B, q % CHUNKS_B
+
+        @on_core(gl)
+        def _():
+            wait_for(fin_b.at[i, z], b_got.at[i])
+            ring_start(fin_b, i, b_ring.at[i], b_up, b_down)
 
     def b_forward(q):
-        ring_forward(fin_b, q, b_send.at[2, q], b_up, b_down, b_far)
+        i = q % CHUNKS_B
+
+        @on_core(q // CHUNKS_B)
+        def _():
+            ring_forward(fin_b, i, b_ring.at[i], b_up, b_down, b_far)
 
     def b_finish(q):
-        ring_finish(fin_b, q, b_up, b_down, b_far, q in DIRECT_B)
+        i = q % CHUNKS_B
+
+        @on_core(q // CHUNKS_B)
+        def _():
+            ring_finish(fin_b, i, b_far)
 
     def a_begin(q):
-        z_a[q, z] = packed[:, :, pl.ds(0, SLOTS_A), pl.ds(q * ROWS_A, ROWS_A)]
+        rows = pl.ds(q % CHUNKS_A * ROWS_A, ROWS_A)
+        z_a[q, z] = packed[:, q // CHUNKS_A, pl.ds(0, SLOTS_A), rows]
         ring_start(z_a, q, a_send.at[0, q], a_up, a_down)
 
     def a_forward(q):
         ring_forward(z_a, q, a_send.at[0, q], a_up, a_down, a_far)
 
     def a_route(q):
-        ring_finish(z_a, q, a_up, a_down, a_far)
+        gl, i = q // CHUNKS_A, q % CHUNKS_A
+        ring_finish(z_a, q, a_far)
         sort(z_a, s_a, q)
-        across(lambda d, gl: s_a.at[q, d, gl], fin_a.at[q, t], a_send.at[1, q], a_got.at[q])
+        across(lambda d: s_a.at[q, d], fin_a.at[i, t], a_send.at[1, q], a_got.at[i], gl)
 
     def a_finish(q):
-        wait_for(fin_a.at[q], a_got.at[q])
+        i = q % CHUNKS_A
+
+        @on_core(q // CHUNKS_A)
+        def _():
+            wait_for(fin_a.at[i], a_got.at[i])
 
     def c_begin(_):
         for d in range(1, SECTIONS):
@@ -216,7 +227,8 @@
 
     def c_route(_):
         wait_for(z_c.at[pl.ds(0, SECTIONS - 1)], c_in)
-        across(lambda d, gl: z_c, fin_c.at[t], c_send.at[1], c_got)
+        for gl in range(GROUPS):
+            across(lambda d: z_c, fin_c.at[t], c_send.at[1 + gl], c_got, gl)
 
     def c_finish(_):
         wait_for(fin_c, c_got)
@@ -254,15 +266,17 @@
         name = item.rstrip("0123456789")
         work[name](int(item[len(name) :] or 0))
 
-    for q in range(CHUNKS_B):
+    for q in range(GROUPS * CHUNKS_B):
         wait_for(z_b.at[q, pl.ds(0, SECTIONS - 1)], b_send.at[0, q])
-        across_sent(fin_b.at[q, z], b_send.at[1, q])
-        wait_for(fin_b.at[q, pl.ds(0, 3)], b_send.at[2, q])
-    for q in range(CHUNKS_A):
+        across_sent(s_b.at[q], b_send.at[1, q], q // CHUNKS_B)
+    for i in range(CHUNKS_B):
+        wait_for(fin_b.at[i, pl.ds(0, 3)], b_ring.at[i])
+    for q in range(GROUPS * CHUNKS_A):
         wait_for(z_a.at[q, pl.ds(0, 3)], a_send.at[0, q])
-        across_sent(fin_a.at[q], a_send.at[1, q])
+        across_sent(s_a.at[q], a_send.at[1, q], q // CHUNKS_A)
     wait_for(z_c.at[pl.ds(0, SECTIONS - 1)], c_send.at[0])
-    across_sent(fin_c, c_send.at[1])
+    for gl in range(GROUPS):
+        across_sent(fin_c, c_send.at[1 + gl], gl)
     stage.wait()
 
 
@@ -274,6 +288,7 @@
     bf = jnp.bfloat16
     hbm, smem, vmem = pltpu.HBM, pltpu.SMEM, pltpu.VMEM
     ca, cb = CHUNKS_A, CHUNKS_B
+    na, nb = GROUPS * ca, GROUPS * cb
     dma = pltpu.SemaphoreType.DMA
     return pl.pallas_call(
         push_kernel,
@@ -291,16 +306,16 @@
             *[vmem((GROUPS, 2 * ROW_BLOCKS, BLK, BLK), jnp.float32)] * OWN,
             vmem((OWN, GROUPS, KEEP, BLK, BLK), bf),
             vmem((WINDOW, WINDOW, 16, BLK), bf),
-            vmem((ca, SECTIONS, OWN, GROUPS, SLOTS_A, ROWS_A, BLK), bf),
-            vmem((ca, EXPERTS, GROUPS, OWN, SLOTS_A, ROWS_A, BLK), bf),
-            vmem((cb, SECTIONS, OWN, GROUPS, ROWS_B, BLK), bf),
-            vmem((cb, EXPERTS, GROUPS, OWN, ROWS_B, BLK), bf),
+            vmem((na, SECTIONS, OWN, SLOTS_A, ROWS_A, BLK), bf),
+            vmem((na, EXPERTS, OWN, SLOTS_A, ROWS_A, BLK), bf),
+            vmem((nb, SECTIONS, OWN, ROWS_B, BLK), bf),
+            vmem((nb, EXPERTS, OWN, ROWS_B, BLK), bf),
             vmem((SECTIONS, 1, BLK), jnp.int32),
             dma((OWN, 4 * GROUPS)),
             dma,
-            *[dma((2, ca)), dma((ca,)), dma((ca,)), dma((ca,)), dma((ca,))],
-            *[dma((3, cb)), dma((cb,)), dma((cb,)), dma((cb,)), dma((cb,)), dma((cb,))],
-            *[dma((2,)), dma, dma],
+            *[dma((2, na)), dma((na,)), dma((na,)), dma((na,)), dma((ca,))],
+            *[dma((2, nb)), dma((cb,)), dma((nb,)), dma((cb,)), dma((cb,)), dma((cb,)), dma((cb,))],
+            *[dma((3,)), dma, dma],
         ],
         compiler_params=pltpu.CompilerParams(
             collective_id=0, has_side_effects=True, vmem_limit_bytes=45 << 20

time: 38.1 us -> 37.9 us (level)
  no operation moved by 1% of the time
where the time goes in v4:
time: 37.9 us; the launch traced here: 37.8 us
  Pallas kernels  37.1 us (98%)
  between operations  0.67 us (2%)
    pallas_call x1, Pallas kernels, push(): pl.pallas_call(push_kernel, out_shape=(vmem(residual.shape, jnp.float32),...  32.2 us
    pallas_call x1, Pallas kernels, apply(): pl.pallas_call(apply_kernel, out_shape=(jax.ShapeDtypeStruct(served.shape...  4.9 us

profile of v4, /device:TPU:1, one launch (start us, length us, event | category | flops | bytes accessed | tf_op | source)
XLA Modules:
  0.0 37.8 jit_solution(13261723523991467960)
XLA Ops:
  0.6 0.0 copy-start
  0.6 0.0 copy-start.1
  0.7 32.2 %push.1 = (f32[2,896,512]{2,1,0:T(8,128)S(1)}, bf16[2,7168,256]{2,1,0:T(8,128)(2,1)S(1)}, bf16[1,8,2,1,128,128]{5,4,3,2,1,0:T(8,128)(2,1)S(1)}, bf16[3,4,8,2,32,...) custom-call(bf16[2,7,128,512]{3,2,1,0:T(8,128)(2,1)} %bitcast.3, f32[2,7,128,512]{3,2,1,0:T(8,128)} %bitcast.2, ...), custom_call_target="tpu_custom_call" | custom-call | tf_op jit(solution)/shard_map/push/pallas_call | solution.py:293
  32.9 0.0 copy-done
  32.9 0.0 copy-done.1
  32.9 4.9 %apply.1 = (bf16[1,2,7168,256]{3,2,1,0:T(8,128)(2,1)}, f32[2,896,512]{2,1,0:T(8,128)}, bf16[2,7168,256]{2,1,0:T(8,128)(2,1)S(1)}) custom-call(s32[8,4,1,128]{3,2,1,0:T(1,128)S(1)} %get-tuple-element.9.codes, s32[8]{0:T(128)S(1)} %copy-done, s32[8]{0:T(128)S(1)} %copy-done.1, ...), custom_call_target="tpu_custom_call", output_to_operand_aliasing={{2}: (4, {})} | custom-call | tf_op jit(solution)/shard_map/apply/pallas_call | solution.py:381
Async XLA Ops:
  0.6 32.3 %copy-start = (s32[8]{0:T(128)S(1)}, s32[8]{0:T(128)}, u32[]{:S(2)}) copy-start(s32[8]{0:T(128)} %count.3) | copy-start | bytes 100
  0.6 32.3 %copy-start.1 = (s32[8]{0:T(128)S(1)}, s32[8]{0:T(128)}, u32[]{:S(2)}) copy-start(s32[8]{0:T(128)} %slots.3) | copy-start | bytes 100

commit v5 on v4

--- a/solution.py
+++ b/solution.py
@@ -324,10 +324,21 @@
     )(by_rows(update), by_rows(residual), kept, count, slots, served)
 
 
-def apply_kernel(codes, count, slots, rest, staged_in, fin_a, fin_b, out, rest_out, staged, sem, rest_sem):
+def apply_kernel(
+    codes_in, count_in, slots_in, rest, staged_in, fin_a, fin_b, out, rest_out, staged,
+    codes, count, slots, sem, rest_sem, small_sem,
+):
     del staged_in
     rest_copy = pltpu.make_async_copy(rest, rest_out, rest_sem)
     rest_copy.start()
+    small = [
+        pltpu.make_async_copy(src, dst, small_sem.at[i])
+        for i, (src, dst) in enumerate(((codes_in, codes), (count_in, count), (slots_in, slots)))
+    ]
+    for copy in small:
+        copy.start()
+    for copy in small:
+        copy.wait()
     _, x, t = own_place()
 
     def region(place, source):
@@ -385,9 +396,13 @@
             jax.ShapeDtypeStruct(rest.shape, rest.dtype),
             vmem(staged.shape, staged.dtype),
         ),
-        in_specs=[pl.BlockSpec(memory_space=smem)] * 3 + [pl.BlockSpec(memory_space=vmem)] * 4,
+        in_specs=[pl.BlockSpec(memory_space=pl.ANY)] * 3 + [pl.BlockSpec(memory_space=vmem)] * 4,
         out_specs=[pl.BlockSpec(memory_space=m) for m in (pltpu.HBM, pltpu.HBM, vmem)],
-        scratch_shapes=[pltpu.SemaphoreType.DMA] * 2,
+        scratch_shapes=[
+            *[smem(a.shape, a.dtype) for a in (codes, count, slots)],
+            *[pltpu.SemaphoreType.DMA] * 2,
+            pltpu.SemaphoreType.DMA((3,)),
+        ],
         input_output_aliases={4: 2},
         compiler_params=pltpu.CompilerParams(vmem_limit_bytes=32 << 20),
         name="apply",

time: 37.9 us -> 37.2 us (0.982)
  Pallas kernels: 37.1 us -> 36.3 us
    pallas_call x1, Pallas kernels: 4.9 us -> 4.12 us  [apply(): pl.pallas_call(apply_kernel, out_shape=(jax.ShapeDtypeStruct(served.shape...]
where the time goes in v5:
time: 37.2 us; the launch traced here: 37 us
  Pallas kernels  36.3 us (98%)
  between operations  0.67 us (2%)
    pallas_call x1, Pallas kernels, push(): pl.pallas_call(push_kernel, out_shape=(vmem(residual.shape, jnp.float32),...  32.2 us
    pallas_call x1, Pallas kernels, apply(): pl.pallas_call(apply_kernel, out_shape=(jax.ShapeDtypeStruct(served.shape...  4.12 us

profile of v5, /device:TPU:1, one launch (start us, length us, event | category | flops | bytes accessed | tf_op | source)
XLA Modules:
  0.0 37.0 jit_solution(2726839487730444502)
XLA Ops:
  0.6 0.0 copy-start
  0.6 0.0 copy-start.1
  0.7 32.2 %push.1 = (f32[2,896,512]{2,1,0:T(8,128)S(1)}, bf16[2,7168,256]{2,1,0:T(8,128)(2,1)S(1)}, bf16[1,8,2,1,128,128]{5,4,3,2,1,0:T(8,128)(2,1)S(1)}, bf16[3,4,8,2,32,...) custom-call(bf16[2,7,128,512]{3,2,1,0:T(8,128)(2,1)} %bitcast.3, f32[2,7,128,512]{3,2,1,0:T(8,128)} %bitcast.2, ...), custom_call_target="tpu_custom_call" | custom-call | tf_op jit(solution)/shard_map/push/pallas_call | solution.py:293
  32.9 0.0 copy-done
  32.9 0.0 copy-done.1
  32.9 4.1 %apply.1 = (bf16[1,2,7168,256]{3,2,1,0:T(8,128)(2,1)}, f32[2,896,512]{2,1,0:T(8,128)}, bf16[2,7168,256]{2,1,0:T(8,128)(2,1)S(1)}) custom-call(s32[8,4,1,128]{3,2,1,0:T(1,128)S(1)} %get-tuple-element.9.codes_in, s32[8]{0:T(128)S(1)} %copy-done, s32[8]{0:T(128)S(1)} %copy-done.1, ...), custom_call_target="tpu_custom_call", output_to_operand_aliasing={{2}: (4, {})} | custom-call | tf_op jit(solution)/shard_map/apply/pallas_call | solution.py:392
Async XLA Ops:
  0.6 32.3 %copy-start = (s32[8]{0:T(128)S(1)}, s32[8]{0:T(128)}, u32[]{:S(2)}) copy-start(s32[8]{0:T(128)} %count_in.1) | copy-start | bytes 100
  0.6 32.3 %copy-start.1 = (s32[8]{0:T(128)S(1)}, s32[8]{0:T(128)}, u32[]{:S(2)}) copy-start(s32[8]{0:T(128)} %slots_in.1) | copy-start | bytes 100

commit v6 on v5

--- a/solution.py
+++ b/solution.py
@@ -43,11 +43,11 @@
 
 
 def push_kernel(
-    update, residual, kept, count, slots, served,
+    update, residual, kept_in, count_in, slots_in, served,
     res_out, staged, fin_a, fin_b, fin_c,
     upd_0, upd_1, rest_0, rest_1, packed, sel, z_a, s_a, z_b, s_b, z_c,
     load_sem, stage_sem, a_send, a_up, a_down, a_far, a_got, b_send, b_ring, b_in, b_got, b_up, b_down, b_far,
-    c_send, c_in, c_got,
+    c_send, c_in, c_got, kept, count, slots, small_sem,
 ):
     z, x, t = own_place()
     up, down = ((z + 1) % SECTIONS, x, t), ((z + 3) % SECTIONS, x, t)
@@ -67,6 +67,12 @@
         else:
             greet()
 
+    small = [
+        pltpu.make_async_copy(src, dst, small_sem.at[i])
+        for i, (src, dst) in enumerate(((kept_in, kept), (count_in, count), (slots_in, slots)))
+    ]
+    for copy in small:
+        copy.start()
     upd, rest = (upd_0, upd_1), (rest_0, rest_1)
     loads = [[] for _ in range(OWN)]
     for le in range(OWN):
@@ -81,6 +87,8 @@
     for load in (*loads[0], *loads[1]):
         load.start()
 
+    for copy in small:
+        copy.wait()
     for p in range(WINDOW):
         for e in range(WINDOW):
             here = (slots[e] == p).astype(jnp.float32)
@@ -299,7 +307,7 @@
             vmem((cb, SECTIONS, TENSORS, OWN, ROWS_B, BLK), bf),
             vmem((TENSORS, SECTIONS, 1, BLK), jnp.int32),
         ),
-        in_specs=[pl.BlockSpec(memory_space=m) for m in (hbm, hbm, smem, smem, smem, hbm)],
+        in_specs=[pl.BlockSpec(memory_space=m) for m in (hbm, hbm, pl.ANY, pl.ANY, pl.ANY, hbm)],
         out_specs=(pl.BlockSpec(memory_space=vmem),) * 5,
         scratch_shapes=[
             *[vmem((GROUPS, 2 * ROW_BLOCKS, BLK, BLK), bf)] * OWN,
@@ -316,6 +324,8 @@
             *[dma((2, na)), dma((na,)), dma((na,)), dma((na,)), dma((ca,))],
             *[dma((2, nb)), dma((cb,)), dma((nb,)), dma((cb,)), dma((cb,)), dma((cb,)), dma((cb,))],
             *[dma((3,)), dma, dma],
+            *[smem(a.shape, a.dtype) for a in (kept, count, slots)],
+            dma((3,)),
         ],
         compiler_params=pltpu.CompilerParams(
             collective_id=0, has_side_effects=True, vmem_limit_bytes=45 << 20

time: 37.2 us -> 36.5 us (0.981)
  Pallas kernels: 36.3 us -> 35.7 us
    pallas_call x1, Pallas kernels: 32.2 us -> 31.5 us  [push(): pl.pallas_call(push_kernel, out_shape=(vmem(residual.shape, jnp.float32),...]
where the time goes in v6:
time: 36.5 us; the launch traced here: 36.3 us
  Pallas kernels  35.7 us (98%)
  between operations  0.67 us (2%)
    pallas_call x1, Pallas kernels, push(): pl.pallas_call(push_kernel, out_shape=(vmem(residual.shape, jnp.float32),...  31.5 us
    pallas_call x1, Pallas kernels, apply(): pl.pallas_call(apply_kernel, out_shape=(jax.ShapeDtypeStruct(served.shape...  4.12 us

profile of v6, /device:TPU:1, one launch (start us, length us, event | category | flops | bytes accessed | tf_op | source)
XLA Modules:
  0.0 36.3 jit_solution(18194620648833581545)
XLA Ops:
  0.6 0.0 copy-start
  0.6 0.0 copy-start.1
  0.7 31.5 %push.1 = (f32[2,896,512]{2,1,0:T(8,128)S(1)}, bf16[2,7168,256]{2,1,0:T(8,128)(2,1)S(1)}, bf16[1,8,2,1,128,128]{5,4,3,2,1,0:T(8,128)(2,1)S(1)}, bf16[3,4,8,2,32,...) custom-call(bf16[2,7,128,512]{3,2,1,0:T(8,128)(2,1)} %bitcast.3, f32[2,7,128,512]{3,2,1,0:T(8,128)} %bitcast.2, ...), custom_call_target="tpu_custom_call" | custom-call | tf_op jit(solution)/shard_map/push/pallas_call | solution.py:301
  32.2 0.0 copy-done
  32.2 0.0 copy-done.1
  32.2 4.1 %apply.1 = (bf16[1,2,7168,256]{3,2,1,0:T(8,128)(2,1)}, f32[2,896,512]{2,1,0:T(8,128)}, bf16[2,7168,256]{2,1,0:T(8,128)(2,1)S(1)}) custom-call(s32[8,4,1,128]{3,2,1,0:T(1,128)S(1)} %get-tuple-element.9.codes_in, s32[8]{0:T(128)S(1)} %copy-done, s32[8]{0:T(128)S(1)} %copy-done.1, ...), custom_call_target="tpu_custom_call", output_to_operand_aliasing={{2}: (4, {})} | custom-call | tf_op jit(solution)/shard_map/apply/pallas_call | solution.py:402
Async XLA Ops:
  0.6 31.6 %copy-start = (s32[8]{0:T(128)S(1)}, s32[8]{0:T(128)}, u32[]{:S(2)}) copy-start(s32[8]{0:T(128)} %count_in.3) | copy-start | bytes 100
  0.6 31.6 %copy-start.1 = (s32[8]{0:T(128)S(1)}, s32[8]{0:T(128)}, u32[]{:S(2)}) copy-start(s32[8]{0:T(128)} %slots_in.3) | copy-start | bytes 100
